TPU v7x, 128 devices: a whole 4x4x4 slice. The times are simulated.
128 devices in a mesh: group: 2 (over x_hi), seq: 8 (over y, x_lo), tp: 8 (over z, core).
Axes of the slice: x: 4 (x_hi: 2, x_lo: 2; x = x_hi * 2 + x_lo), y: 4, z: 4, core: 2. Of those that a mesh axis runs over, the one named last changes fastest.
Arguments:
- prompt_tokens: bfloat16 [2, 4096, 5120], P(None, ('group', 'seq')), may hold values from -6 to 6
- prompt_lengths: int32 [2], replicated, may hold values from 1024 to 4096
- prompt_token_start: int32 [2], replicated, may hold values from 0 to 12287
- block_owner: int32 [128, 2, 1], P(('group', 'seq')), may hold values from 0 to 15; in each aligned block of 16 rows (0 to 15, 16 to 31, ..., all dimensions but the last counted through in order) at most 2 rows name the same one
- decode_hidden: bfloat16 [128, 4, 5120], P(('group', 'seq')), may hold values from -6 to 6
- cache_lengths: int32 [128], P(('group', 'seq')), may hold values from 1 to 1024
- key_cache: bfloat16 [128, 1024, 1024], P(('group', 'seq'), None, 'tp'), may hold values from -6 to 6
- value_cache: bfloat16 [128, 1024, 1024], P(('group', 'seq'), None, 'tp'), may hold values from -6 to 6
- w_query: bfloat16 [5120, 4096], P(None, 'tp'), may hold values from -0.078125 to 0.078125
- w_key: bfloat16 [5120, 1024], P(None, 'tp'), may hold values from -0.078125 to 0.078125
- w_value: bfloat16 [5120, 1024], P(None, 'tp'), may hold values from -0.078125 to 0.078125
- w_out: bfloat16 [4096, 5120], P('tp'), may hold values from -0.5 to 0.5
- query_gain: float32 [128], replicated, may hold values from 0.5 to 8
- key_gain: float32 [128], replicated, may hold values from 0.5 to 8
Outputs:
- prefill_context: bfloat16 [2, 4096, 4096], P(None, ('group', 'seq'), 'tp')
- kv_pool: bfloat16 [16, 32, 32, 2, 1024], P(('group', 'seq'), None, None, None, 'tp')
- decode_out: bfloat16 [128, 4, 5120], P(('group', 'seq'))
Inputs may be any that keep to these rules, and one draw needn't show every extreme that they name: `block_owner`: in the rows of one index of group and seq (16 rows), no owner is named more than 2 times.
All inputs are finite; a program needn't handle non-finite values.
Results may differ from a plain program's by a relative error of at most 0.019.
The roundings to bfloat16 on the way count: a program that leaves them out, or rounds other values in their place, can miss the bound.
Values may be sent and summed in bfloat16 or wider, within the bound.
A program may use at most 192 MiB of HBM per device.

v0:
```python
import jax
import jax.numpy as jnp
from jax import lax
from jax.sharding import PartitionSpec as P

BLK = 32


eps = 1e-06
theta = 1000000.0


def head_norm(raw, gain):
    mean_sq = jnp.mean(raw * raw, axis=-1, keepdims=True)
    return raw * lax.rsqrt(mean_sq + eps) * gain


def rotate(raw, positions):
    half = raw.shape[-1] // 2
    freqs = theta ** (-jnp.arange(half, dtype=jnp.float32) * 2.0 / raw.shape[-1])
    angles = positions[..., None, None] * freqs
    cosine = jnp.cos(angles)
    sine = jnp.sin(angles)
    first = raw[..., :half]
    second = raw[..., half:]
    return jnp.concatenate(
        [first * cosine - second * sine, second * cosine + first * sine], axis=-1
    )


def project(hidden, weight, heads, gain, positions):
    raw = jnp.dot(hidden.reshape(-1, hidden.shape[-1]), weight, preferred_element_type=jnp.float32)
    raw = raw.reshape(hidden.shape[:-1] + (heads, -1))
    return rotate(head_norm(raw, gain), positions).astype(jnp.bfloat16)


def plain_values(hidden, weight, heads):
    raw = jnp.dot(hidden.reshape(-1, hidden.shape[-1]), weight, preferred_element_type=jnp.float32)
    return raw.astype(jnp.bfloat16).reshape(hidden.shape[:-1] + (heads, -1))


def block_ranks(owners):
    count = owners.shape[-1]
    earlier = jnp.tril(jnp.ones((count, count), jnp.int32), -1)
    same = (owners[..., :, None] == owners[..., None, :]).astype(jnp.int32)
    return jnp.sum(same * earlier, axis=-1)


def per_device(
    prompt_tokens,
    prompt_lengths,
    prompt_token_start,
    block_owner,
    decode_hidden,
    cache_lengths,
    key_cache,
    value_cache,
    w_query,
    w_key,
    w_value,
    w_out,
    query_gain,
    key_gain,
):
    prompts, local_len, width = prompt_tokens.shape
    head_dim = query_gain.shape[0]
    kv_heads = w_key.shape[1] // head_dim
    q_heads = w_query.shape[1] // head_dim
    group_size = q_heads // kv_heads
    kv_width = kv_heads * head_dim
    scale = head_dim ** (-0.5)
    n_group = lax.axis_size("group")
    n_seq = lax.axis_size("seq")
    shards = n_group * n_seq
    here = lax.axis_index(("group", "seq"))
    token_pos = here * local_len + jnp.arange(local_len, dtype=jnp.int32)
    positions = (
        prompt_token_start[:, None].astype(jnp.float32) + token_pos.astype(jnp.float32)[None, :]
    )
    queries = project(prompt_tokens, w_query, q_heads, query_gain, positions)
    keys = project(prompt_tokens, w_key, kv_heads, key_gain, positions)
    values = plain_values(prompt_tokens, w_value, kv_heads)
    keys_flat = keys.reshape(prompts, local_len, kv_width)
    values_flat = values.reshape(prompts, local_len, kv_width)
    q_grouped = queries.reshape(prompts, local_len, kv_heads, group_size, head_dim)
    start_top = jnp.full((prompts, kv_heads, group_size, local_len), -jnp.inf, jnp.float32)
    start_total = jnp.zeros((prompts, kv_heads, group_size, local_len), jnp.float32)
    start_acc = jnp.zeros((prompts, kv_heads, group_size, local_len, head_dim), jnp.float32)
    start_carry = (start_top, start_total, start_acc)
    top = start_carry[0]
    total = start_carry[1]
    acc = start_carry[2]
    key_piece = lax.all_gather(keys_flat, ("group", "seq"), axis=1, tiled=True).reshape(
        prompts, -1, kv_heads, head_dim
    )
    value_piece = lax.all_gather(values_flat, ("group", "seq"), axis=1, tiled=True).reshape(
        prompts, -1, kv_heads, head_dim
    )
    count = key_piece.shape[1]
    key_pos = jnp.arange(count, dtype=jnp.int32)
    scores = (
        jnp.einsum("pqngd,pknd->pngqk", q_grouped, key_piece, preferred_element_type=jnp.float32)
        * scale
    )
    allowed = (key_pos[None, None, :] <= token_pos[None, :, None]) & (
        key_pos[None, None, :] < prompt_lengths[:, None, None]
    )
    scores = jnp.where(allowed[:, None, None], scores, -jnp.inf)
    new_top = jnp.max(scores, axis=-1)
    safe_top = jnp.where(new_top == -jnp.inf, 0.0, new_top)
    weights = jnp.exp(scores - safe_top[..., None])
    scale_correction = jnp.exp(top - safe_top)
    total = total * scale_correction + jnp.sum(weights, axis=-1)
    update = jnp.einsum(
        "pngqk,pknd->pngqd",
        weights.astype(jnp.bfloat16),
        value_piece,
        preferred_element_type=jnp.float32,
    )
    acc = acc * scale_correction[..., None] + update
    context = acc / total[..., None]
    context = context.transpose(0, 3, 1, 2, 4).reshape(prompts, local_len, q_heads * head_dim)
    valid = token_pos[None, :] < prompt_lengths[:, None]
    prefill_context = jnp.where(valid[..., None], context, 0.0).astype(jnp.bfloat16)
    blocks_here = block_owner.shape[0] * block_owner.shape[1]
    capacity = 2 * blocks_here // shards
    slot_ids = jnp.arange(capacity, dtype=jnp.int32)
    stacked_pieces = jnp.stack([keys_flat, values_flat], axis=2)
    block_list = stacked_pieces.reshape(prompts, local_len // BLK, BLK, 2, kv_width).transpose(
        1, 0, 2, 3, 4
    )
    owners = block_owner.reshape(-1)
    block_list = block_list.reshape(blocks_here, BLK * 2 * kv_width)
    ranks = block_ranks(owners)
    target_index = jnp.arange(shards, dtype=jnp.int32)
    choose_entries = (owners[None, None, :] == target_index[:, None, None]) & (
        ranks[None, None, :] == slot_ids[None, :, None]
    )
    outgoing = jnp.einsum(
        "phv,vl->phl",
        choose_entries.astype(jnp.bfloat16),
        block_list,
        preferred_element_type=jnp.float32,
    ).astype(jnp.bfloat16)
    outgoing = outgoing.reshape(shards, capacity, BLK, 2, kv_width)
    received = lax.all_to_all(outgoing, ("group", "seq"), split_axis=0, concat_axis=0, tiled=True)
    kv_pool = received.reshape(1, shards * capacity, BLK, 2, kv_width)
    rows, steps, _ = decode_hidden.shape
    cache_slots = key_cache.shape[1]
    new_pos = (
        cache_lengths[:, None].astype(jnp.float32) + jnp.arange(steps, dtype=jnp.float32)[None, :]
    )
    dq = project(decode_hidden, w_query, q_heads, query_gain, new_pos)
    dk = project(decode_hidden, w_key, kv_heads, key_gain, new_pos)
    dv = plain_values(decode_hidden, w_value, kv_heads)
    all_keys = jnp.concatenate(
        [key_cache.reshape(rows, cache_slots, kv_heads, head_dim), dk], axis=1
    )
    all_values = jnp.concatenate(
        [value_cache.reshape(rows, cache_slots, kv_heads, head_dim), dv], axis=1
    )
    dq_grouped = dq.reshape(rows, steps, kv_heads, group_size, head_dim)
    scores = (
        jnp.einsum("rsngd,rknd->rngsk", dq_grouped, all_keys, preferred_element_type=jnp.float32)
        * scale
    )
    slot = jnp.arange(cache_slots + steps, dtype=jnp.int32)
    step = jnp.arange(steps, dtype=jnp.int32)
    allowed = jnp.where(
        slot[None, None, :] < cache_slots,
        slot[None, None, :] < cache_lengths[:, None, None],
        slot[None, None, :] - cache_slots <= step[None, :, None],
    )
    scores = jnp.where(allowed[:, None, None], scores, -jnp.inf)
    top = jnp.max(scores, axis=-1, keepdims=True)
    weights = jnp.exp(scores - top)
    total = jnp.sum(weights, axis=-1)
    mixed = (
        jnp.einsum(
            "rngsk,rknd->rngsd",
            weights.astype(jnp.bfloat16),
            all_values,
            preferred_element_type=jnp.float32,
        )
        / total[..., None]
    )
    decode_context = (
        mixed.transpose(0, 3, 1, 2, 4)
        .reshape(rows * steps, q_heads * head_dim)
        .astype(jnp.bfloat16)
    )
    partial_out = jnp.dot(decode_context, w_out, preferred_element_type=jnp.float32)
    summed = lax.psum(partial_out.astype(jnp.bfloat16), "tp")
    decode_out = summed.reshape(rows, steps, -1)
    return (prefill_context, kv_pool, decode_out)


def solution(mesh):
    placed = (
        P(None, ("group", "seq"), None),
        P(),
        P(),
        P(("group", "seq"), None, None),
        P(("group", "seq"), None, None),
        P(("group", "seq")),
        P(("group", "seq"), None, "tp"),
        P(("group", "seq"), None, "tp"),
        P(None, "tp"),
        P(None, "tp"),
        P(None, "tp"),
        P("tp", None),
        P(),
        P(),
    )
    return jax.shard_map(
        per_device,
        mesh=mesh,
        in_specs=placed,
        out_specs=(
            P(None, ("group", "seq"), "tp"),
            P(("group", "seq"), None, None, None, "tp"),
            P(("group", "seq"), None, None),
        ),
        check_vma=False,
    )
```

profile of v0, /device:TPU:30, one launch (start us, length us, event | category | flops | bytes accessed | tf_op | source)
XLA Modules:
  0.0 201.9 jit_solution(5427611002096394407)
XLA Ops:
  8.1 1.2 copy-done
  9.3 4.2 %multiply_reduce_fusion.1 = (f32[512]{0:T(512)S(1)}, f32[512,128]{1,0:T(8,128)S(1)}) fusion(bf16[512,5120]{1,0:T(8,128)(2,1)} %bitcast.147, bf16[5120,128]{1,0:T(8,128)(2,1)S(1)} %copy-done), kind=kOutput, calls=%fused_computation.62 | convolution fusion | flops 671219200 | bytes 6817792 | tf_op jit(solution)/shard_map/dot_general | solution.py:32
  13.6 0.1 multiply_multiply_fusion.1
  13.8 1.2 fusion.48
  15.0 0.8 pad_maximum_fusion
  15.8 4.0 %convolution_convert_fusion.2 = bf16[512,128]{1,0:T(8,128)(2,1)S(1)} fusion(bf16[512,5120]{1,0:T(8,128)(2,1)} %bitcast.148, bf16[5120,128]{1,0:T(8,128)(2,1)S(1)} %copy-done.2), kind=kOutput, calls=%fused_computation.30 | convolution fusion | flops 671154176 | bytes 6684672 | tf_op jit(solution)/shard_map/dot_general | solution.py:38
  19.8 0.1 maximum_bitcast_fusion.8
  19.9 0.3 copy.50
  20.2 0.2 reshape.631
  20.4 0.1 copy.49
  20.5 0.1 eq.67
  20.6 0.2 select_reduce_fusion
  20.8 0.3 convolution_convert_fusion
  21.1 0.4 reshape.616
  21.4 1.3 copy.51
  22.7 7.1 %all-to-all-start = ((bf16[16,2,32,2,128]{4,3,2,1,0:T(2,128)(2,1)}), bf16[16,2,32,2,128]{4,3,2,1,0:T(2,128)(2,1)}, u32[]{:S(2)}, u32[]{:S(2)}) async-start(bf16[16,2,32,2,128]{4,3,2,1,0:T(2,128)(2,1)} %copy.51), calls=%async_computation | async-start | bytes 1048576 | tf_op jit(solution)/shard_map/all_to_all | solution.py:146
  29.9 0.8 copy.46
  30.8 8.2 %copy.62 = bf16[512,5120]{1,0:T(8,128)(2,1)} copy(bf16[512,5120]{0,1:T(8,128)(2,1)} %bitcast.131) | data formatting | bytes 10485760 | tf_op jit(solution)/shard_map/dot_general | solution.py:32
  39.1 4.3 %multiply_reduce_fusion.2 = (f32[8,4,4]{1,2,0:T(4,128)S(1)}, f32[8,4,4,128]{3,1,2,0:T(4,128)S(1)}) fusion(bf16[4,128,5120,1]{2,1,0,3:T(8,128)(2,1)} %bitcast.134, bf16[8,4,5120]{2,1,0:T(4,128)(2,1)S(1)} %copy-done.4), kind=kOutput, calls=%fused_computation.70 | convolution fusion | flops 167804800 | bytes 5636608 | tf_op jit(solution)/shard_map/dot_general | solution.py:32
  43.4 0.4 multiply_reduce_fusion.3
  43.9 0.1 rsqrt.42
  44.0 0.2 multiply_cosine_fusion.2
  44.2 0.1 multiply_multiply_fusion.2
  44.3 0.1 subtract_convert_fusion.1
  44.4 0.1 pad_maximum_fusion.1
  44.6 0.2 fusion.59
  45.0 2.7 %fusion.72 = (f32[8,4,4]{1,2,0:T(4,128)S(1)}, f32[8,1,4,4,1028]{4,2,3,0,1:T(4,128)S(1)}) fusion(bf16[8,4,4,128]{3,1,2,0:T(4,128)(2,1)S(1)} %pad_maximum_fusion.1, bf16[8,4,1,64]{3,1,0,2:T(4,128)(2,1)S(1)} %get-tuple-element.10, bf16[8,4,1,64]{3,1,0,2:T(4,128)(2,1)S(1)} %get-tuple-element.9, bf16[8,1024,1,128]{3,1,0,2:T(8,128)(2,1)} %bitcast.149, ...), kind=kOutput, calls=%fused_computation.120 | convolution fusion | flops 40396160 | bytes 2697856 | tf_op jit(solution)/shard_map/rsngd,rknd->rngsk/dot_general | solution.py:164
  47.6 0.4 fusion.36
  48.0 0.3 convolution_convert_fusion.3
  48.3 0.6 fusion.32
  49.0 1.0 convolution_convert_fusion.1
  50.0 0.9 reshape.626
  50.9 6.5 %multiply_reduce_fusion = (f32[2,256,4]{1,2,0:T(4,128)S(1)}, f32[2,256,4,128]{1,3,2,0:T(8,128)S(1)}) fusion(bf16[4,128,5120,1]{2,1,0,3:T(8,128)(2,1)} %bitcast.135, bf16[2,256,5120]{2,1,0:T(8,128)(2,1)} %param.14), kind=kOutput, calls=%fused_computation.37 | convolution fusion | flops 2684876800 | bytes 11542528 | tf_op jit(solution)/shard_map/dot_general | solution.py:32
  57.4 0.7 iota_compare_fusion
  58.2 0.1 iota_compare_fusion.2
  58.3 0.2 multiply_multiply_fusion
  58.5 2.2 %broadcast_and_fusion = pred[2,256,4096]{1,2,0:T(8,128)(4,1)S(1)} fusion(pred[2,4096]{1,0:T(4,128)(4,1)S(1)} %iota_compare_fusion.2, pred[256,4096]{0,1:T(8,128)(4,1)S(1)} %iota_compare_fusion), kind=kLoop, calls=%fused_computation.13 | loop fusion | flops 2097152 | bytes 3153920 | tf_op jit(solution)/shard_map/and | solution.py:105
  60.7 0.5 multiply_cosine_fusion.1
  61.2 0.1 subtract_convert_fusion
  61.4 34.1 %all-gather.3.cloned.1.call-done = bf16[2,4096,128]{2,1,0:T(8,128)(2,1)} async-done(((bf16[2,256,128]{2,1,0:T(8,128)(2,1)}), bf16[2,4096,128]{2,1,0:T(8,128)(2,1)}) %all-gather.3.cloned.1.call-update) | async-done | bytes 2097168 | tf_op jit(solution)/shard_map/all_gather | solution.py:93
  95.5 14.9 %fusion.2 = (f32[2,4,256]{2,1,0:T(4,128)S(1)}, f32[2,4096,256,4]{2,1,3,0:T(8,128)}) fusion(pred[2,256,4096]{1,2,0:T(8,128)(4,1)S(1)} %broadcast_and_fusion, bf16[2,256,4,64]{1,3,2,0:T(8,128)(2,1)S(1)} %get-tuple-element.4, bf16[2,256,4,64]{1,3,2,0:T(8,128)(2,1)S(1)} %get-tuple-element.3, bf16[2,4096,128]{2,1,0:T(8,128)(2,1)} %all-gather.3.cloned.1.call-done), kind=kOutput, calls=%fused_computation.4 | convolution fusion | flops 2173696000 | bytes 38281216 | tf_op jit(solution)/shard_map/pqngd,pknd->pngqk/dot_general | solution.py:102
  110.4 14.6 %fusion = f32[2,4,256]{2,1,0:T(4,128)S(1)} fusion(f32[2,4096,256,4]{2,1,3,0:T(8,128)} %get-tuple-element.22, f32[2,4,256]{2,1,0:T(4,128)S(1)} %compare_select_fusion, pred[2,256,4096]{1,2,0:T(8,128)(4,1)S(1)} %broadcast_and_fusion), kind=kLoop, calls=%fused_computation.2 | loop fusion | flops 33552384 | bytes 35667968 | tf_op jit(solution)/shard_map/reduce_sum | solution.py:113
  125.0 47.3 %all-gather.5.cloned.1.call-done = bf16[2,4096,128]{1,2,0:T(8,128)(2,1)} async-done(((bf16[2,256,128]{1,2,0:T(8,128)(2,1)}), bf16[2,4096,128]{1,2,0:T(8,128)(2,1)}) %all-gather.5.cloned.1.call-update) | async-done | bytes 2097168 | tf_op jit(solution)/shard_map/all_gather | solution.py:96
  172.3 15.8 %fusion.26 = bf16[2,4,256,128]{2,3,1,0:T(8,128)(2,1)} fusion(f32[2,4096,256,4]{2,1,3,0:T(8,128)} %get-tuple-element.22, f32[2,4,256]{2,1,0:T(4,128)S(1)} %compare_select_fusion, pred[2,256,4096]{1,2,0:T(8,128)(4,1)S(1)} %broadcast_and_fusion, bf16[2,4096,128]{1,2,0:T(8,128)(2,1)} %all-gather.5.cloned.1.call-done, f32[2,4,256]{2,1,0:T(4,128)S(1)} %get-tuple-element.12, ...), kind=kOutput, calls=%fused_computation.31 | convolution fusion | flops 2181824512 | bytes 38297600 | tf_op jit(solution)/shard_map/pngqk,pknd->pngqd/dot_general | solution.py:114
  188.1 1.3 copy.48
  189.4 1.0 select_convert_fusion
  190.4 2.3 %copy.74 = bf16[1,32,32,2,128]{4,3,2,1,0:T(2,128)(2,1)} copy(bf16[1,32,32,2,128]{4,3,2,1,0:T(2,128)(2,1)} %bitcast.23) | data formatting | bytes 1048576
  192.6 1.8 copy.75
  (61 shorter events, 0.9 us)
Async XLA Ops:
  8.0 1.3 copy-start
  8.0 5.5 %copy-start.11 = (s32[2]{0:T(128)S(1)}, s32[2]{0:T(128)}, u32[]{:S(2)}) copy-start(s32[2]{0:T(128)} %param.16) | copy-start | bytes 28
  8.0 5.6 %copy-start.5 = (f32[128]{0:T(128)S(1)}, f32[128]{0:T(128)}, u32[]{:S(2)}) copy-start(f32[128]{0:T(128)} %param.27) | copy-start | bytes 1540
  8.0 87.5 %all-gather.3.cloned.1.call-start = ((), (), s32[]{:S(2)}) async-start(), calls=%async_computation.1 | async-start | bytes 2228224 | tf_op jit(solution)/shard_map/all_gather | solution.py:93
  9.3 6.5 %copy-start.2 = (bf16[5120,128]{1,0:T(8,128)(2,1)S(1)}, bf16[5120,128]{1,0:T(8,128)(2,1)}, u32[]{:S(2)}) copy-start(bf16[5120,128]{1,0:T(8,128)(2,1)} %param.24) | copy-start | bytes 3932164
  15.8 4.6 %copy-start.8 = (s32[8,2,1]{0,2,1:T(1,128)S(1)}, s32[8,2,1]{0,2,1:T(1,128)}, u32[]{:S(2)}) copy-start(s32[8,2,1]{0,2,1:T(1,128)} %param.17) | copy-start | bytes 196
  19.8 10.9 %copy-start.9 = (s32[8]{0:T(128)S(1)}, s32[8]{0:T(128)}, u32[]{:S(2)}) copy-start(s32[8]{0:T(128)} %param.19) | copy-start | bytes 100
  22.7 38.7 %all-to-all-start = ((bf16[16,2,32,2,128]{4,3,2,1,0:T(2,128)(2,1)}), bf16[16,2,32,2,128]{4,3,2,1,0:T(2,128)(2,1)}, u32[]{:S(2)}, u32[]{:S(2)}) async-start(bf16[16,2,32,2,128]{4,3,2,1,0:T(2,128)(2,1)} %copy.51), calls=%async_computation | async-start | bytes 1048576 | tf_op jit(solution)/shard_map/all_to_all | solution.py:146
  29.8 142.5 %all-gather.5.cloned.1.call-start = ((), (), s32[]{:S(2)}) async-start(), calls=%async_computation.2 | async-start | bytes 2228224 | tf_op jit(solution)/shard_map/all_gather | solution.py:96
  30.7 159.7 %all-reduce.2.cloned.1.call-start = ((), (), s32[]{:S(2)}) async-start(), calls=%async_computation.3 | async-start | bytes 655360 | tf_op jit(solution)/shard_map/psum | solution.py:193
  30.8 8.2 %copy-start.4 = (bf16[8,4,5120]{2,1,0:T(4,128)(2,1)S(1)}, bf16[8,4,5120]{2,1,0:T(4,128)(2,1)}, u32[]{:S(2)}) copy-start(bf16[8,4,5120]{2,1,0:T(4,128)(2,1)} %param.18) | copy-start | bytes 983044
  39.1 5.1 %copy-start.6 = (f32[128]{0:T(128)S(1)}, f32[128]{0:T(128)}, u32[]{:S(2)}) copy-start(f32[128]{0:T(128)} %param.26) | copy-start | bytes 1540
  43.9 4.1 %copy-start.3 = (bf16[5120,128]{1,0:T(8,128)(2,1)S(1)}, bf16[5120,128]{1,0:T(8,128)(2,1)}, u32[]{:S(2)}) copy-start(bf16[5120,128]{1,0:T(8,128)(2,1)} %param.24) | copy-start | bytes 3932164
  44.9 4.1 %slice-start = ((s8[5242880]{0:T(1024)(128)(4,1)}), s8[4194304]{0:T(1024)(128)(4,1)S(1)}, s32[]{:S(2)}) async-start(s8[5242880]{0:T(1024)(128)(4,1)} %bitcast.132), calls=%async_computation.4 | async-start | bytes 8388608
  44.9 3.4 %copy-start.10 = (bf16[8,1024,128]{2,1,0:T(8,128)(2,1)S(1)}, bf16[8,1024,128]{2,1,0:T(8,128)(2,1)}, u32[]{:S(2)}) copy-start(bf16[8,1024,128]{2,1,0:T(8,128)(2,1)} %param.21) | copy-start | bytes 6291460
  45.0 4.0 %slice-start.1 = ((s8[5242880]{0:T(1024)(128)(4,1)}), s8[1048576]{0:T(1024)(128)(4,1)S(1)}, s32[]{:S(2)}) async-start(s8[5242880]{0:T(1024)(128)(4,1)} %bitcast.132), calls=%async_computation.5 | async-start | bytes 2097152
  50.9 7.3 %copy-start.7 = (s32[2]{0:T(128)S(1)}, s32[2]{0:T(128)}, u32[]{:S(2)}) copy-start(s32[2]{0:T(128)} %param.15) | copy-start | bytes 28
  172.3 22.1 %copy-start.1 = (bf16[5120,128]{1,0:T(8,128)(2,1)S(1)}, bf16[5120,128]{1,0:T(8,128)(2,1)}, u32[]{:S(2)}) copy-start(bf16[5120,128]{1,0:T(8,128)(2,1)} %param.23) | copy-start | bytes 3932164
Sparse Core Ops, SparseCore 0:
  15.9 79.5 all-gather.2
  97.1 75.1 all-gather.4
Sparse Core Ops, SparseCore 1:
  51.0 63.4 all-reduce.1
where the time goes:
time: 205 us; the launch traced here: 202 us
  waiting for transfers between devices  81.5 us (40%)
  matrix products  55 us (27%)
  other arithmetic  23.4 us (11%)
  local copies, waits for them, and re-layouts  18.9 us (9%)
  between operations  15.9 us (8%)
  starting transfers between devices  7.21 us (4%)
    all_gather x1, waiting for transfers between devices, per_device(): lax.all_gather(values_flat, ('group', 'seq'), axis=1, tiled=True)  47.3 us
    all_gather x1, waiting for transfers between devices, per_device(): lax.all_gather(keys_flat, ('group', 'seq'), axis=1, tiled=True)  34.1 us
    dot_general x1, matrix products, per_device(): jnp.einsum('pngqk,pknd->pngqd', weights.astype(jnp.bfloat16), value_piece...  15.8 us
    dot_general x4, matrix products, project(): jnp.dot(hidden.reshape(-1, hidden.shape[-1]), weight, preferred_element_t...  15.4 us
    dot_general x1, matrix products, per_device(): jnp.einsum('pqngd,pknd->pngqk', q_grouped, key_piece, preferred_element_t...  14.9 us
    reduce_sum x1, other arithmetic, per_device(): total = total * scale_correction + jnp.sum(weights, axis=-1)  14.6 us
    dot_general x1, local copies, waits for them, and re-layouts, project(): jnp.dot(hidden.reshape(-1, hidden.shape[-1]), weight, preferred_element_t...  8.19 us
    all_to_all x1, starting transfers between devices, per_device(): lax.all_to_all(outgoing, ('group', 'seq'), split_axis=0, concat_axis=0, t...  7.09 us
  transfers between devices with their start and end apart: 4, of which 2 were waited for; matrix products, arithmetic and copies ran while one was open for 42% of the time, Pallas kernels for 0%

commit v1 on v0

v1 whole, which is shorter than its diff:
```python
import numpy as np
import jax
import jax.numpy as jnp
from jax import lax
from jax.experimental import pallas as pl
from jax.experimental.pallas import tpu as pltpu
from jax.sharding import PartitionSpec as P

MESH = pl.DeviceIdType.MESH
F32 = jnp.float32
BF16 = jnp.bfloat16
I32 = jnp.int32

EPS = 1e-06
THETA = 1000000.0
HD = 128
TOK = 256
NP = 2
ROWS = NP * TOK
NH = 4
DR = 8
ST = 4
DT = DR * ST
D = 5120
CACHE = 1024
NS = 16
KCH = 1024
NKC = D // KCH
PIECE = D // 8
SM = HD**-0.5 * 1.4426950408889634

ORDER = [
    (0, 0),
    (3, 0), (1, 0), (0, 3), (0, 1),
    (2, 0), (0, 2),
    (3, 3), (1, 1), (3, 1), (1, 3),
    (3, 2), (1, 2), (2, 3), (2, 1),
    (2, 2),
]
STEP = {o: k for k, o in enumerate(ORDER)}


def rem(a, b):
    return lax.rem(a, b if a.ndim == 0 else jnp.full(a.shape, b, a.dtype))


def div(a, b):
    return lax.div(a, b if a.ndim == 0 else jnp.full(a.shape, b, a.dtype))


def nt(a, b):
    return lax.dot_general(a, b, (((1,), (1,)), ((), ())), preferred_element_type=F32)


def mm(a, b):
    return jnp.dot(a, b, preferred_element_type=F32)


def iota(shape, dim):
    return lax.broadcasted_iota(I32, shape, dim)


def norm_rope(raw, gain, cosine, sine):
    mean_sq = jnp.mean(raw * raw, axis=-1, keepdims=True)
    u = raw * lax.rsqrt(mean_sq + EPS) * gain
    return (u * cosine + pltpu.roll(u, HD // 2, 1) * sine).astype(BF16)


def kernel(
    start_ref, len_ref, owner_ref, clen_ref,
    freq_ref, cosb_ref, sinb_ref, qg_ref, kg_ref,
    x_hbm, hd_hbm, kc_hbm, vc_hbm, wq_hbm, wk_hbm, wv_hbm, wo_hbm,
    ctx_hbm, pool_hbm, dec_hbm,
    xs, hd, kc, vc, wq, wkv, wo,
    kvacc, qacc, cosf, sinf, dcos, dsin,
    G, Qs, M, L, ACC, dk, dv, dq,
    CT, CS, PI, pool, ctxs,
    PS, RS, DO,
    in_sem, out_sem, send_sem, recv_sem, tsend_sem, trecv_sem, ct_sem,
    rs_send, rs_recv, ag_send, ag_recv,
):
    g = lax.axis_index("group")
    s = lax.axis_index("seq")
    t = lax.axis_index("tp")
    X = g * 2 + rem(s, 2)
    Y = div(s, 2)
    me = g * 8 + s

    place = {}
    for dx, dy in ORDER:
        xx = rem(X + dx, 4)
        yy = rem(Y + dy, 4)
        place[dx, dy] = div(xx, 2), yy * 2 + rem(xx, 2)
    place_shard = {o: gg * 8 + ss for o, (gg, ss) in place.items()}
    num = [g * 0 + i for i in range(64)]
    tps = [rem(t + i, 8) for i in range(8)]
    tp_cols = [pl.ds(pl.multiple_of(u * PIECE, HD), PIECE) for u in tps]

    def at(dx, dy):
        return place[dx, dy]

    def shard(dx, dy):
        return place_shard[dx, dy]

    loads = []

    def load(src, dst, n):
        c = pltpu.make_async_copy(src, dst, in_sem.at[n])
        c.start()
        return c

    n = 0
    first = []
    for i in range(NKC):
        ks = pl.ds(i * KCH, KCH)
        first.append((
            load(x_hbm.at[:, ks], xs.at[pl.ds(0, ROWS), ks], n),
            load(wk_hbm.at[ks, :], wkv.at[ks, pl.ds(0, HD)], n + 1),
            load(wv_hbm.at[ks, :], wkv.at[ks, pl.ds(HD, HD)], n + 2),
        ))
        n += 3
        if i == 0:
            hd_load = load(hd_hbm, hd, n)
            n += 1
    wq_load = []
    for i in range(NKC):
        ks = pl.ds(i * KCH, KCH)
        wq_load.append(load(wq_hbm.at[ks, :], wq.at[ks, :], n))
        n += 1
    kc_load = load(kc_hbm, kc, n)
    vc_load = load(vc_hbm, vc, n + 1)
    wo_load = load(wo_hbm, wo, n + 2)

    bar = pltpu.get_barrier_semaphore()
    peers = [at(dx, dy) for dx, dy in ORDER[1:]]
    for gg, ss in peers:
        pl.semaphore_signal(bar, inc=1, device_id=(gg, ss, t), device_id_type=MESH)
    for i in range(1, 8):
        pl.semaphore_signal(bar, inc=1, device_id=(g, s, tps[i]), device_id_type=MESH)

    freq = freq_ref[...]
    sign = jnp.where(iota((1, HD), 1) < HD // 2, -1.0, 1.0).astype(F32)
    for p in range(NP):
        base = (start_ref[p] + me * TOK).astype(F32) * freq
        ca = jnp.cos(base)
        sa = jnp.sin(base) * sign
        cb = cosb_ref[...]
        sb = sinb_ref[...]
        rows = pl.ds(p * TOK, TOK)
        cosf[rows, :] = cb * ca - sb * sa
        sinf[rows, :] = cb * sa + sb * ca
    row = iota((DT, HD), 0)
    pos = rem(row, ST)
    for r in range(DR):
        pos = pos + jnp.where(div(row, ST) == r, clen_ref[r], 0)
    ang = pos.astype(F32) * freq
    dcos[...] = jnp.cos(ang)
    dsin[...] = jnp.sin(ang) * sign

    lane = iota((8, HD), 1)
    want_o = div(lane, 2)
    want_r = rem(lane, 2)
    table = jnp.full((8, HD), -1, I32)
    seen = jnp.zeros((8, HD), I32)
    for v in range(NS):
        hit = want_o == owner_ref[v % 2, v // 2]
        table = jnp.where(hit & (seen == want_r), v, table)
        seen = seen + hit.astype(I32)
    CT[me] = table

    ro = iota((HD, HD), 0)
    co = iota((HD, HD), 1)
    src = div(ro, 64) * 64 + rem(ro, 2) * 32 + div(rem(ro, 64), 2)
    PI[...] = jnp.where(co == src, 1.0, 0.0).astype(BF16)

    hd_load.wait()
    xs[pl.ds(ROWS, DT), :] = hd[...].astype(F32).reshape(DT, D).astype(BF16)

    for i in range(NKC):
        for c in first[i]:
            c.wait()
        ks = pl.ds(i * KCH, KCH)
        part = mm(xs[:, ks], wkv[ks, :])
        if i == 0:
            kvacc[...] = part
        else:
            kvacc[...] += part
    kg = kg_ref[...]
    for p in range(NP):
        rows = pl.ds(p * TOK, TOK)
        G[me, p, 0] = norm_rope(kvacc[rows, :HD], kg, cosf[rows, :], sinf[rows, :])
        G[me, p, 1] = kvacc[rows, HD:].astype(BF16)
    drows = pl.ds(ROWS, DT)
    dk[...] = norm_rope(kvacc[drows, :HD], kg, dcos[...], dsin[...])
    dv[...] = kvacc[drows, HD:].astype(BF16)

    pl.semaphore_wait(bar, len(peers) + 7)

    sends = []

    def rid(k, p, half):
        return (k * 2 + p) * 2 + half

    def send(dx, dy, p, half, to):
        k = STEP[((dx - to[0]) % 4, (dy - to[1]) % 4)]
        j = shard(dx, dy)
        ref = G.at[j, num[p]] if half is None else G.at[j, num[p], num[half]]
        gg, ss = at(*to)
        c = pltpu.make_async_remote_copy(
            src_ref=ref, dst_ref=ref,
            send_sem=send_sem.at[num[len(sends)]],
            recv_sem=recv_sem.at[num[rid(k, p, half or 0)]],
            device_id=(gg, ss, t), device_id_type=MESH,
        )
        sends.append(c)
        c.start()

    def arrive(k, p, half):
        j = shard(*ORDER[k])
        ref = G.at[j, num[p]] if half is None else G.at[j, num[p], num[half]]
        pltpu.make_async_remote_copy(
            src_ref=ref, dst_ref=ref, send_sem=send_sem.at[num[0]],
            recv_sem=recv_sem.at[num[rid(k, p, half or 0)]],
            device_id=(g, s, t), device_id_type=MESH,
        ).wait_recv()

    def flip(o, p):
        return o if p == 0 else (o[1], o[0])

    def comm(k):
        for p in range(NP):
            a, b = flip(ORDER[k], p)
            o = ORDER[k]
            if a == 2 and b == 0 or b == 2:
                arrive(k, p, 0)
                arrive(k, p, 1)
            else:
                arrive(k, p, None)
            if b == 0 and a in (1, 3):
                send(*o, p, 0 if a == 3 else 1, flip((4 - a, 0), p))
            if b == 0:
                send(*o, p, None, flip((0, 1), p))
                send(*o, p, None, flip((0, 3), p))
            if b in (1, 3):
                send(*o, p, 0 if b == 3 else 1, flip((0, 4 - b), p))

    for p in range(NP):
        for d in (1, 3):
            send(0, 0, p, None, flip((d, 0), p))
    for p in range(NP):
        for d in (1, 3):
            send(0, 0, p, None, flip((0, d), p))

    tsends = []
    for i, (dx, dy) in enumerate(ORDER[1:]):
        gg, ss = at(dx, dy)
        k = STEP[((-dx) % 4, (-dy) % 4)]
        c = pltpu.make_async_remote_copy(
            src_ref=CT.at[me], dst_ref=CT.at[me],
            send_sem=tsend_sem.at[num[i]], recv_sem=trecv_sem.at[num[k]],
            device_id=(gg, ss, t), device_id_type=MESH,
        )
        c.start()
        tsends.append(c)

    for i in range(NKC):
        wq_load[i].wait()
        ks = pl.ds(i * KCH, KCH)
        part = mm(xs[:, ks], wq[ks, :])
        if i == 0:
            qacc[...] = part
        else:
            qacc[...] += part
    qg = qg_ref[...]
    for h in range(NH):
        cols = pl.ds(h * HD, HD)
        for p in range(NP):
            rows = pl.ds(p * TOK, TOK)
            Qs[p, h] = norm_rope(qacc[rows, cols], qg, cosf[rows, :], sinf[rows, :])
        dq[:, cols] = norm_rope(qacc[drows, cols], qg, dcos[...], dsin[...])

    def attend(p, h, j, own):
        q = Qs[p, h]
        sc = nt(q, G[j, p, 0])
        if own:
            sc = jnp.where(iota((TOK, TOK), 1) <= iota((TOK, TOK), 0), sc, -1e30)
        s0 = sc[:, :HD]
        s1 = sc[:, HD:]
        top = jnp.max(jnp.maximum(s0, s1), axis=1, keepdims=True)
        if own:
            new = jnp.broadcast_to(top, (TOK, HD))
        else:
            old = M[p, h]
            new = jnp.maximum(old, top)
        mb = new * SM
        p0 = jnp.exp2(s0 * SM - mb)
        p1 = jnp.exp2(s1 * SM - mb)
        w = jnp.concatenate([p0.astype(BF16), p1.astype(BF16)], axis=1)
        o = mm(w, G[j, p, 1])
        M[p, h] = new
        if own:
            L[p, h] = p0 + p1
            ACC[p, h] = o
        else:
            alpha = jnp.exp2(old * SM - mb)
            L[p, h] = L[p, h] * alpha + (p0 + p1)
            ACC[p, h] = ACC[p, h] * alpha + o

    def blocks(j):
        rows = []
        for r in range(2):
            code = CS[j, 0, me * 2 + r]
            kb = jnp.zeros((32, HD), BF16)
            vb = jnp.zeros((32, HD), BF16)
            for v in range(NS):
                here = code == v
                span = pl.ds((v // 2) * 32, 32)
                kb = jnp.where(here, G[j, v % 2, 0, span, :], kb)
                vb = jnp.where(here, G[j, v % 2, 1, span, :], vb)
            rows += [kb, vb]
        both = jnp.concatenate(rows, axis=0)
        pool[j] = mm(PI[...], both).astype(BF16)

    for p in range(NP):
        for h in range(NH):
            attend(p, h, me, True)

    for k in (1, 2, 3, 4):
        comm(k)

    kc_load.wait()
    vc_load.wait()
    er = iota((HD, DT), 0)
    ec = iota((HD, DT), 1)
    same = div(er, 16) == div(ec, ST)
    qd = jnp.zeros((HD, HD), F32)
    for h in range(NH):
        pick = same & (rem(er, ST) == rem(ec, ST)) & (rem(div(er, ST), NH) == h)
        qd = qd + mm(jnp.where(pick, 1.0, 0.0).astype(BF16), dq[:, h * HD:(h + 1) * HD])
    qd = qd.astype(BF16)
    sn = nt(qd, dk[...])
    sn = jnp.where(same & (rem(ec, ST) <= rem(er, ST)), sn, -1e30)
    outs = []
    for r in range(DR):
        span = slice(r * 16, r * 16 + 16)
        sr = nt(qd[span], kc[r])
        sr = jnp.where(iota((16, CACHE), 1) < clen_ref[r], sr, -1e30)
        top = jnp.maximum(
            jnp.max(sr, axis=1, keepdims=True), jnp.max(sn[span], axis=1, keepdims=True)
        )
        wr = jnp.exp2((sr - top) * SM)
        wn = jnp.exp2((sn[span] - top) * SM)
        total = jnp.sum(wr, axis=1, keepdims=True) + jnp.sum(wn, axis=1, keepdims=True)
        mixed = mm(wr.astype(BF16), vc[r]) + mm(wn.astype(BF16), dv[...])
        outs.append(mixed / total)
    cd = jnp.concatenate(outs, axis=0).astype(BF16)
    tr = iota((DT, HD), 0)
    tc = iota((DT, HD), 1)
    heads = []
    for h in range(NH):
        pick = (div(tc, 16) == div(tr, ST)) & (rem(tc, ST) == rem(tr, ST)) & (rem(div(tc, ST), NH) == h)
        heads.append(mm(jnp.where(pick, 1.0, 0.0).astype(BF16), cd).astype(BF16))
    dctx = jnp.concatenate(heads, axis=1)
    wo_load.wait()
    for i in range(8):
        PS[i] = mm(dctx, wo[:, i * PIECE:(i + 1) * PIECE]).astype(BF16)
    rsends = []
    for i in range(1, 8):
        to = tps[i]
        c = pltpu.make_async_remote_copy(
            src_ref=PS.at[to], dst_ref=RS.at[t],
            send_sem=rs_send.at[num[i]], recv_sem=rs_recv.at[num[8 - i]],
            device_id=(g, s, to), device_id_type=MESH,
        )
        c.start()
        rsends.append(c)

    for k in range(1, NS):
        j = shard(*ORDER[k])
        pltpu.make_async_remote_copy(
            src_ref=CT.at[j], dst_ref=CT.at[j], send_sem=tsend_sem.at[num[0]],
            recv_sem=trecv_sem.at[num[k]], device_id=(g, s, t), device_id_type=MESH,
        ).wait_recv()
    ctc = pltpu.make_async_copy(CT, CS, ct_sem)
    ctc.start()
    ctc.wait()
    blocks(me)

    asends = []
    mine = tp_cols[0]

    def reduce():
        total = PS[t].astype(F32)
        for i in range(1, 8):
            frm = tps[i]
            pltpu.make_async_remote_copy(
                src_ref=PS.at[frm], dst_ref=RS.at[frm], send_sem=rs_send.at[num[0]],
                recv_sem=rs_recv.at[num[i]], device_id=(g, s, t), device_id_type=MESH,
            ).wait_recv()
            total = total + RS[frm].astype(F32)
        DO[:, mine] = total.astype(BF16)
        for i in range(1, 8):
            c = pltpu.make_async_remote_copy(
                src_ref=DO.at[:, mine], dst_ref=DO.at[:, mine],
                send_sem=ag_send.at[num[i]], recv_sem=ag_recv.at[num[8 - i]],
                device_id=(g, s, tps[i]), device_id_type=MESH,
            )
            c.start()
            asends.append(c)

    @pl.loop(1, NS)
    def _(kk):
        j = 0
        for k in range(1, NS):
            j = j + jnp.where(kk == k, shard(*ORDER[k]), 0)
            if k > 4:
                @pl.when(kk == k)
                def _():
                    comm(k)

        @pl.when(kk == 5)
        def _():
            reduce()

        @pl.when(j < me)
        def _():
            for p in range(NP):
                for h in range(NH):
                    attend(p, h, j, False)
        blocks(j)

    pool_out = pltpu.make_async_copy(pool, pool_hbm, out_sem.at[0])
    pool_out.start()

    for i in range(1, 8):
        frm = tps[i]
        cols = tp_cols[i]
        pltpu.make_async_remote_copy(
            src_ref=DO.at[:, cols], dst_ref=DO.at[:, cols], send_sem=ag_send.at[num[0]],
            recv_sem=ag_recv.at[num[i]], device_id=(g, s, t), device_id_type=MESH,
        ).wait_recv()
    dec_out = pltpu.make_async_copy(DO, dec_hbm, out_sem.at[1])
    dec_out.start()

    for p in range(NP):
        tok = me * TOK + iota((TOK, HD), 0)
        keep = tok < len_ref[p]
        for h in range(NH):
            total = jnp.sum(L[p, h], axis=1, keepdims=True)
            out = jnp.where(keep, ACC[p, h] / total, 0.0)
            ctxs[pl.ds(p * TOK, TOK), pl.ds(h * HD, HD)] = out.astype(BF16)
    ctx_out = pltpu.make_async_copy(ctxs, ctx_hbm, out_sem.at[2])
    ctx_out.start()
    for c in sends + tsends + rsends + asends:
        c.wait_send()
    pool_out.wait()
    dec_out.wait()
    ctx_out.wait()


def tables():
    freq = THETA ** (-np.arange(HD // 2, dtype=np.float64) * 2.0 / HD)
    ang = np.arange(TOK, dtype=np.float64)[:, None] * freq[None, :]
    cosb = np.concatenate([np.cos(ang), np.cos(ang)], axis=1).astype(np.float32)
    sinb = np.concatenate([-np.sin(ang), np.sin(ang)], axis=1).astype(np.float32)
    freq = np.concatenate([freq, freq])[None, :].astype(np.float32)
    return freq, cosb, sinb


def per_device(
    prompt_tokens, prompt_lengths, prompt_token_start, block_owner, decode_hidden,
    cache_lengths, key_cache, value_cache, w_query, w_key, w_value, w_out,
    query_gain, key_gain,
):
    freq, cosb, sinb = (jnp.asarray(a) for a in tables())
    vm = pl.BlockSpec(memory_space=pltpu.VMEM)
    sm = pl.BlockSpec(memory_space=pltpu.SMEM)
    hbm = pl.BlockSpec(memory_space=pl.ANY)
    V = pltpu.VMEM
    ctx, pool, dec = pl.pallas_call(
        kernel,
        out_shape=(
            jax.ShapeDtypeStruct((ROWS, NH * HD), BF16),
            jax.ShapeDtypeStruct((NS, HD, HD), BF16),
            jax.ShapeDtypeStruct((DT, D), BF16),
        ),
        in_specs=[sm] * 4 + [vm] * 5 + [hbm] * 8,
        out_specs=(hbm, hbm, hbm),
        scratch_shapes=[
            V((ROWS + DT, D), BF16),
            V((DR, ST, D), BF16),
            V((DR, CACHE, HD), BF16),
            V((DR, CACHE, HD), BF16),
            V((D, NH * HD), BF16),
            V((D, 2 * HD), BF16),
            V((NH * HD, D), BF16),
            V((ROWS + DT, 2 * HD), F32),
            V((ROWS + DT, NH * HD), F32),
            V((ROWS, HD), F32),
            V((ROWS, HD), F32),
            V((DT, HD), F32),
            V((DT, HD), F32),
            V((NS, NP, 2, TOK, HD), BF16),
            V((NP, NH, TOK, HD), BF16),
            V((NP, NH, TOK, HD), F32),
            V((NP, NH, TOK, HD), F32),
            V((NP, NH, TOK, HD), F32),
            V((DT, HD), BF16),
            V((DT, HD), BF16),
            V((DT, NH * HD), BF16),
            V((NS, 8, HD), I32),
            pltpu.SMEM((NS, 8, HD), I32),
            V((HD, HD), BF16),
            V((NS, HD, HD), BF16),
            V((ROWS, NH * HD), BF16),
            V((8, DT, PIECE), BF16),
            V((8, DT, PIECE), BF16),
            V((DT, D), BF16),
            pltpu.SemaphoreType.DMA((32,)),
            pltpu.SemaphoreType.DMA((3,)),
            pltpu.SemaphoreType.DMA((64,)),
            pltpu.SemaphoreType.DMA((64,)),
            pltpu.SemaphoreType.DMA((16,)),
            pltpu.SemaphoreType.DMA((16,)),
            pltpu.SemaphoreType.DMA,
            pltpu.SemaphoreType.DMA((8,)),
            pltpu.SemaphoreType.DMA((8,)),
            pltpu.SemaphoreType.DMA((8,)),
            pltpu.SemaphoreType.DMA((8,)),
        ],
        compiler_params=pltpu.CompilerParams(
            collective_id=0, has_side_effects=True, vmem_limit_bytes=58 * 1024 * 1024
        ),
        name="split_attention",
    )(
        prompt_token_start, prompt_lengths,
        block_owner.transpose(1, 2, 0).reshape(NP, 8), cache_lengths,
        freq, cosb, sinb,
        query_gain.reshape(1, HD), key_gain.reshape(1, HD),
        prompt_tokens.reshape(ROWS, D), decode_hidden, key_cache, value_cache,
        w_query, w_key, w_value, w_out,
    )
    return (
        ctx.reshape(NP, TOK, NH * HD),
        pool.reshape(1, 2 * NS, 32, 2, HD),
        dec.reshape(DR, ST, D),
    )


def solution(mesh):
    placed = (
        P(None, ("group", "seq"), None),
        P(),
        P(),
        P(("group", "seq"), None, None),
        P(("group", "seq"), None, None),
        P(("group", "seq")),
        P(("group", "seq"), None, "tp"),
        P(("group", "seq"), None, "tp"),
        P(None, "tp"),
        P(None, "tp"),
        P(None, "tp"),
        P("tp", None),
        P(),
        P(),
    )
    return jax.shard_map(
        per_device,
        mesh=mesh,
        in_specs=placed,
        out_specs=(
            P(None, ("group", "seq"), "tp"),
            P(("group", "seq"), None, None, None, "tp"),
            P(("group", "seq"), None, None),
        ),
        check_vma=False,
    )
```

time: 205 us -> 57.6 us (0.28); the launches traced: 202 us -> 57.3 us
  waiting for transfers between devices: 81.5 us -> 0 us
  matrix products: 55 us -> 0 us
  Pallas kernels: 0 us -> 50.7 us
  other arithmetic: 23.4 us -> 0 us
  between operations: 15.9 us -> 0.65 us
  local copies, waits for them, and re-layouts: 18.9 us -> 5.97 us
  starting transfers between devices: 7.21 us -> 0 us
    all_gather x2 -> x0, waiting for transfers between devices: 81.4 us -> none  [the longest x1 47.3 us: per_device(): lax.all_gather(values_flat, ('group', 'seq'), axis=1, tiled=True)]
    dot_general x12 -> x0, matrix products: 55 us -> none  [the longest x1 15.8 us: per_device(): jnp.einsum('pngqk,pknd->pngqd', weights.astype(jnp.bfloat16), value_piece...]
    pallas_call x0 -> x1, Pallas kernels: none -> 50.7 us  [per_device(): pl.pallas_call(kernel, out_shape=(jax.ShapeDtypeStruct((ROWS, NH * HD), B...]
    reduce_sum x3 -> x0, other arithmetic: 15.1 us -> none  [the longest x1 14.6 us: per_device(): total = total * scale_correction + jnp.sum(weights, axis=-1)]
    dot_general x1 -> x0, local copies, waits for them, and re-layouts: 8.19 us -> none  [project(): jnp.dot(hidden.reshape(-1, hidden.shape[-1]), weight, preferred_element_t...]
    all_to_all x1 -> x0, starting transfers between devices: 7.09 us -> none  [per_device(): lax.all_to_all(outgoing, ('group', 'seq'), split_axis=0, concat_axis=0, t...]
    reshape x6 -> x1, local copies, waits for them, and re-layouts: 4.03 us -> 1.82 us  [per_device(): dec.reshape(DR, ST, D)]
    and x1 -> x0, other arithmetic: 2.15 us -> none  [per_device(): (key_pos[None, None, :] <= token_pos[None, :, None]) & (key_pos[None, Non...]
  transfers between devices with their start and end apart: 4 -> 0, of which waited for: 2 -> 0; matrix products, arithmetic and copies ran while one was open for 42% -> 0% of each run, Pallas kernels for 0% -> 0%
where the time goes in v1:
time: 57.6 us; the launch traced here: 57.3 us
  Pallas kernels  50.7 us (88%)
  local copies, waits for them, and re-layouts  5.97 us (10%)
  between operations  0.65 us (1%)
    pallas_call x1, Pallas kernels, per_device(): pl.pallas_call(kernel, out_shape=(jax.ShapeDtypeStruct((ROWS, NH * HD), B...  50.7 us
    unnamed x2, local copies, waits for them, and re-layouts  4.14 us
    reshape x1, local copies, waits for them, and re-layouts, per_device(): dec.reshape(DR, ST, D)  1.82 us

profile of v1, /device:TPU:30, one launch (start us, length us, event | category | flops | bytes accessed | tf_op | source)
XLA Modules:
  0.0 57.3 jit_solution(18044971117843444872)
XLA Ops:
  0.6 50.7 %split_attention.1 = (bf16[512,512]{1,0:T(8,128)(2,1)}, bf16[16,128,128]{2,1,0:T(8,128)(2,1)}, bf16[32,5120]{1,0:T(8,128)(2,1)}) custom-call(s32[2]{0:T(128)} %start_ref.1, s32[2]{0:T(128)} %len_ref.1, s32[2,8]{1,0:T(2,128)} %bitcast.11, s32[8]{0:T(128)} %clen_ref.1, f32[1,128]{1,0:T(1,128)} %constant.6.clone.freq_ref, f32[256,128]{1,0:T(8,128)} %constant.7.clone.cosb_ref, ...), custom_call_target="tpu_custom_call" | custom-call | tf_op jit(solution)/shard_map/split_attention/pallas_call | solution.py:480
  51.4 1.8 %reshape.33 = bf16[8,4,5120]{2,1,0:T(4,128)(2,1)} reshape(bf16[32,5120]{1,0:T(8,128)(2,1)} %get-tuple-element.8) | data formatting | bytes 655360 | tf_op jit(solution)/shard_map/reshape | solution.py:546
  53.2 1.9 %copy.22 = bf16[2,256,512]{2,1,0:T(8,128)(2,1)} copy(bf16[2,256,512]{2,1,0:T(8,128)(2,1)} %bitcast.10) | data formatting | bytes 1048576
  55.1 2.3 %copy.23 = bf16[1,32,32,2,128]{4,3,2,1,0:T(2,128)(2,1)} copy(bf16[1,32,32,2,128]{4,3,2,1,0:T(2,128)(2,1)} %bitcast.9) | data formatting | bytes 1048576

commit v2 on v1

v2 whole, which is shorter than its diff:
```python
import numpy as np
import jax
import jax.numpy as jnp
from jax import lax
from jax.experimental import pallas as pl
from jax.experimental.pallas import tpu as pltpu
from jax.sharding import PartitionSpec as P

MESH = pl.DeviceIdType.MESH
F32 = jnp.float32
BF16 = jnp.bfloat16
I32 = jnp.int32

EPS = 1e-06
THETA = 1000000.0
HD = 128
TOK = 256
NP = 2
ROWS = NP * TOK
NH = 4
DR = 8
ST = 4
DT = DR * ST
D = 5120
CACHE = 1024
NS = 16
CH = 2 * TOK + 16
KCH = 1024
NKC = D // KCH
PIECE = D // 8
SM = HD**-0.5 * 1.4426950408889634

ORDER = [
    (0, 0),
    (3, 0), (1, 0), (0, 3), (0, 1),
    (2, 0), (0, 2),
    (3, 3), (1, 1), (3, 1), (1, 3),
    (3, 2), (1, 2), (2, 3), (2, 1),
    (2, 2),
]
STEP = {o: k for k, o in enumerate(ORDER)}
LATER = {
    3: ((7, 0), (8, 0), (7, 1), (8, 1)),
    4: ((9, 0), (10, 0), (9, 1), (10, 1)),
    5: ((5, 1),),
    6: ((6, 0),),
    8: ((13, 0), (14, 0), (11, 1), (12, 1)),
    11: ((11, 0), (12, 0)),
    13: ((13, 1), (14, 1)),
    15: ((15, 0), (15, 1)),
}


def rem(a, b):
    return lax.rem(a, b) if a.ndim == 0 else a & (b - 1)


def div(a, b):
    return lax.div(a, b) if a.ndim == 0 else lax.shift_right_logical(a, jnp.full(a.shape, b.bit_length() - 1, a.dtype))


def nt(a, b):
    return lax.dot_general(a, b, (((1,), (1,)), ((), ())), preferred_element_type=F32)


def mm(a, b):
    return jnp.dot(a, b, preferred_element_type=F32)


def iota(shape, dim):
    return lax.broadcasted_iota(I32, shape, dim)


def norm_rope(raw, gain, cosine, sine):
    mean_sq = mm((raw * raw).astype(BF16), jnp.full((HD, HD), 1.0 / HD, BF16))
    u = raw * lax.rsqrt(mean_sq + EPS) * gain
    return (u * cosine + pltpu.roll(u, HD // 2, 1) * sine).astype(BF16)


def kernel(
    start_ref, len_ref, owner_ref, clen_ref,
    tab_hbm, qg_hbm, kg_hbm,
    x_hbm, hd_hbm, kc_hbm, vc_hbm, wq_hbm, wk_hbm, wv_hbm, wo_hbm,
    ctx_hbm, pool_hbm, dec_hbm,
    xs, hd, kc, vc, wq, wkv, wo,
    kvacc, qacc, cosf, sinf, dcos, dsin,
    G, Qs, M, L, ACC, dk, dv, dq,
    tab, gains, PI, NUM, pool, ctxs,
    PS, RS, DO,
    in_sem, out_sem, send_sem, recv_sem,
    rs_send, rs_recv, ag_send, ag_recv,
):
    g = lax.axis_index("group")
    s = lax.axis_index("seq")
    t = lax.axis_index("tp")
    X = g * 2 + rem(s, 2)
    Y = div(s, 2)
    me = g * 8 + s

    place = {}
    for dx, dy in ORDER:
        xx = rem(X + dx, 4)
        yy = rem(Y + dy, 4)
        place[dx, dy] = div(xx, 2), yy * 2 + rem(xx, 2)
    place_shard = {o: gg * 8 + ss for o, (gg, ss) in place.items()}
    num = [g * 0 + i for i in range(64)]
    tps = [rem(t + i, 8) for i in range(8)]
    tp_cols = [pl.ds(pl.multiple_of(u * PIECE, HD), PIECE) for u in tps]

    def at(dx, dy):
        return place[dx, dy]

    def shard(dx, dy):
        return place_shard[dx, dy]

    def load(src, dst, n, now=True):
        c = pltpu.make_async_copy(src, dst, in_sem.at[n])
        if now:
            c.start()
        return c

    n = 0
    first = []
    for i in range(NKC):
        ks = pl.ds(i * KCH, KCH)
        first.append((
            load(x_hbm.at[:, ks], xs.at[pl.ds(0, ROWS), ks], n),
            load(wk_hbm.at[ks, :], wkv.at[ks, pl.ds(0, HD)], n + 1),
            load(wv_hbm.at[ks, :], wkv.at[ks, pl.ds(HD, HD)], n + 2),
        ))
        n += 3
        if i == 0:
            hd_load = load(hd_hbm, hd, n)
            small = (
                load(tab_hbm, tab, n + 1),
                load(qg_hbm, gains.at[0], n + 2),
                load(kg_hbm, gains.at[1], n + 3),
            )
            n += 4
    wq_load = []
    for i in range(NKC):
        ks = pl.ds(i * KCH, KCH)
        wq_load.append(load(wq_hbm.at[ks, :], wq.at[ks, :], n, False))
        n += 1
    kc_load = load(kc_hbm, kc, n, False)
    vc_load = load(vc_hbm, vc, n + 1, False)
    wo_load = load(wo_hbm, wo, n + 2, False)

    bar = pltpu.get_barrier_semaphore()
    for o in ((1, 0), (3, 0), (0, 1), (0, 3)):
        gg, ss = at(*o)
        pl.semaphore_signal(bar, inc=1, device_id=(gg, ss, t), device_id_type=MESH)
    for i in range(1, 8):
        pl.semaphore_signal(bar, inc=1, device_id=(g, s, tps[i]), device_id_type=MESH)

    lane = iota((16, HD), 1)
    want_o = div(lane, 2)
    want_r = rem(lane, 2)
    table = jnp.full((16, HD), -1, I32)
    seen = jnp.zeros((16, HD), I32)
    for v in range(NS):
        hit = want_o == owner_ref[v % 2, v // 2]
        table = jnp.where(hit & (seen == want_r), v, table)
        seen = seen + hit.astype(I32)
    for p in range(NP):
        G[me, p, pl.ds(2 * TOK, 16), :] = table.astype(F32).astype(BF16)

    for c in small:
        c.wait()
    freq = tab[pl.ds(2 * TOK, 1), :]
    sign = jnp.where(iota((1, HD), 1) < HD // 2, -1.0, 1.0).astype(F32)
    for p in range(NP):
        base = (start_ref[p] + me * TOK).astype(F32) * freq
        ca = jnp.cos(base)
        sa = jnp.sin(base) * sign
        cb = tab[pl.ds(0, TOK), :]
        sb = tab[pl.ds(TOK, TOK), :]
        rows = pl.ds(p * TOK, TOK)
        cosf[rows, :] = cb * ca - sb * sa
        sinf[rows, :] = cb * sa + sb * ca
    row = iota((DT, HD), 0)
    pos = rem(row, ST)
    for r in range(DR):
        pos = pos + jnp.where(div(row, ST) == r, clen_ref[r], 0)
    ang = pos.astype(F32) * freq
    dcos[...] = jnp.cos(ang)
    dsin[...] = jnp.sin(ang) * sign

    hd_load.wait()
    xs[pl.ds(ROWS, DT), :] = hd[...].astype(F32).reshape(DT, D).astype(BF16)

    for i in range(NKC):
        for c in first[i]:
            c.wait()
        if i >= NKC - 2:
            for c in wq_load[:2] if i == NKC - 2 else wq_load[2:]:
                c.start()
        ks = pl.ds(i * KCH, KCH)
        part = mm(xs[:, ks], wkv[ks, :])
        if i == 0:
            kvacc[...] = part
        else:
            kvacc[...] += part
    kg = gains[1]
    for p in range(NP):
        rows = pl.ds(p * TOK, TOK)
        G[me, p, pl.ds(0, TOK), :] = norm_rope(kvacc[rows, :HD], kg, cosf[rows, :], sinf[rows, :])
        G[me, p, pl.ds(TOK, TOK), :] = kvacc[rows, HD:].astype(BF16)
    drows = pl.ds(ROWS, DT)
    dk[...] = norm_rope(kvacc[drows, :HD], kg, dcos[...], dsin[...])
    dv[...] = kvacc[drows, HD:].astype(BF16)

    def query_part(i):
        wq_load[i].wait()
        ks = pl.ds(i * KCH, KCH)
        part = mm(xs[:, ks], wq[ks, :])
        if i == 0:
            qacc[...] = part
        else:
            qacc[...] += part

    query_part(0)
    query_part(1)
    kc_load.start()
    vc_load.start()

    pl.semaphore_wait(bar, 4 + 7)

    sends = []

    def part_of(j, p, half):
        if half is None:
            return G.at[j, num[p]]
        return G.at[j, num[p], pl.ds(0, TOK) if half == 0 else pl.ds(TOK, CH - TOK)]

    def rid(k, p, half):
        return (k * 2 + p) * 2 + half

    def send(dx, dy, p, half, to):
        k = STEP[((dx - to[0]) % 4, (dy - to[1]) % 4)]
        j = shard(dx, dy)
        ref = part_of(j, p, half)
        gg, ss = at(*to)
        c = pltpu.make_async_remote_copy(
            src_ref=ref, dst_ref=ref,
            send_sem=send_sem.at[num[len(sends)]],
            recv_sem=recv_sem.at[num[rid(k, p, half or 0)]],
            device_id=(gg, ss, t), device_id_type=MESH,
        )
        sends.append(c)
        c.start()

    def arrive(k, p, half):
        j = shard(*ORDER[k])
        ref = part_of(j, p, half)
        pltpu.make_async_remote_copy(
            src_ref=ref, dst_ref=ref, send_sem=send_sem.at[num[0]],
            recv_sem=recv_sem.at[num[rid(k, p, half or 0)]],
            device_id=(g, s, t), device_id_type=MESH,
        ).wait_recv()

    def flip(o, p):
        return o if p == 0 else (o[1], o[0])

    def comm(k, p):
        a, b = flip(ORDER[k], p)
        o = ORDER[k]
        if a == 2 and b == 0 or b == 2:
            arrive(k, p, 0)
            arrive(k, p, 1)
        else:
            arrive(k, p, None)
        if b == 0 and a in (1, 3):
            send(*o, p, 0 if a == 3 else 1, flip((4 - a, 0), p))
        if b == 0:
            send(*o, p, None, flip((0, 1), p))
            send(*o, p, None, flip((0, 3), p))
        if b in (1, 3):
            send(*o, p, 0 if b == 3 else 1, flip((0, 4 - b), p))

    for p in range(NP):
        for d in (1, 3):
            send(0, 0, p, None, flip((d, 0), p))
    for p in range(NP):
        for d in (1, 3):
            send(0, 0, p, None, flip((0, d), p))

    ro = iota((HD, 4 * TOK), 0)
    co = iota((HD, 4 * TOK), 1)
    same_row = (rem(ro, 2) == rem(div(co, TOK), 2)) & (div(rem(ro, 64), 2) == rem(co, 32))
    PI[...] = jnp.where(same_row, 1.0, 0.0).astype(BF16)
    col = iota((16, 4 * TOK), 1)
    number = rem(div(col, 32), 8) * 2 + div(col, 2 * TOK)
    NUM[...] = number.astype(F32)

    for i in range(2, NKC):
        query_part(i)
        if i == 3:
            wo_load.start()
    qg = gains[0]
    for h in range(NH):
        cols = pl.ds(h * HD, HD)
        for p in range(NP):
            rows = pl.ds(p * TOK, TOK)
            Qs[p, h] = norm_rope(qacc[rows, cols], qg, cosf[rows, :], sinf[rows, :])
        dq[:, cols] = norm_rope(qacc[drows, cols], qg, dcos[...], dsin[...])

    bodies = [(p, h) for p in range(NP) for h in range(NH)]

    def attend(j, own):
        def scores(p, h):
            sc = nt(Qs[p, h], G[j, p, pl.ds(0, TOK), :])
            if own:
                sc = jnp.where(iota((TOK, TOK), 1) <= iota((TOK, TOK), 0), sc, -1e30)
            return sc

        def soft(p, h, sc):
            s0 = sc[:, :HD]
            s1 = sc[:, HD:]
            top = jnp.max(jnp.maximum(s0, s1), axis=1, keepdims=True)
            if own:
                new = jnp.broadcast_to(top, (TOK, HD))
            else:
                old = M[p, h]
                new = jnp.maximum(old, top)
            mb = new * SM
            p0 = jnp.exp2(s0 * SM - mb)
            p1 = jnp.exp2(s1 * SM - mb)
            M[p, h] = new
            if own:
                L[p, h] = p0 + p1
                alpha = None
            else:
                alpha = jnp.exp2(old * SM - mb)
                L[p, h] = L[p, h] * alpha + (p0 + p1)
            return jnp.concatenate([p0.astype(BF16), p1.astype(BF16)], axis=1), alpha

        def mix(p, h, w, alpha):
            o = mm(w, G[j, p, pl.ds(TOK, TOK), :])
            ACC[p, h] = o if own else ACC[p, h] * alpha + o

        sc = scores(*bodies[0])
        waiting = None
        for n, b in enumerate(bodies):
            after = scores(*bodies[n + 1]) if n + 1 < len(bodies) else None
            if waiting is not None:
                mix(*waiting)
            waiting = (*b, *soft(*b, sc))
            sc = after
        mix(*waiting)

    def blocks(j):
        row = G[j, 0, pl.ds(2 * TOK, 16), :].astype(F32)
        number = NUM[...]
        picks = []
        for r in range(2):
            code = jnp.sum(jnp.where(lane == me * 2 + r, row, 0.0), axis=1, keepdims=True)
            picks.append(jnp.where(code == number, 1.0, 0.0).astype(BF16))
        for r in range(2):
            half = pl.ds(r * 64, 64)
            pick = PI[half, :] * jnp.concatenate([picks[r]] * 4, axis=0)
            out = mm(pick[:, : 2 * TOK], G[j, 0, pl.ds(0, 2 * TOK), :])
            out += mm(pick[:, 2 * TOK :], G[j, 1, pl.ds(0, 2 * TOK), :])
            pool[j, half, :] = out.astype(BF16)

    for k, p in ((1, 0), (2, 0), (3, 1), (4, 1)):
        comm(k, p)

    attend(me, True)

    kc_load.wait()
    vc_load.wait()
    er = iota((HD, DT), 0)
    ec = iota((HD, DT), 1)
    same = div(er, 16) == div(ec, ST)
    qd = jnp.zeros((HD, HD), F32)
    for h in range(NH):
        pick = same & (rem(er, ST) == rem(ec, ST)) & (rem(div(er, ST), NH) == h)
        qd = qd + mm(jnp.where(pick, 1.0, 0.0).astype(BF16), dq[:, h * HD:(h + 1) * HD])
    qd = qd.astype(BF16)
    sn = nt(qd, dk[...])
    sn = jnp.where(same & (rem(ec, ST) <= rem(er, ST)), sn, -1e30)
    outs = []
    for r in range(DR):
        span = slice(r * 16, r * 16 + 16)
        sr = nt(qd[span], kc[r])
        sr = jnp.where(iota((16, CACHE), 1) < clen_ref[r], sr, -1e30)
        top = jnp.maximum(
            jnp.max(sr, axis=1, keepdims=True), jnp.max(sn[span], axis=1, keepdims=True)
        )
        wr = jnp.exp2((sr - top) * SM)
        wn = jnp.exp2((sn[span] - top) * SM)
        total = jnp.sum(wr, axis=1, keepdims=True) + jnp.sum(wn, axis=1, keepdims=True)
        mixed = mm(wr.astype(BF16), vc[r]) + mm(wn.astype(BF16), dv[...])
        outs.append(mixed / total)
    cd = jnp.concatenate(outs, axis=0).astype(BF16)
    for k, p in ((3, 0), (4, 0), (1, 1), (2, 1)):
        comm(k, p)
    tr = iota((DT, HD), 0)
    tc = iota((DT, HD), 1)
    heads = []
    for h in range(NH):
        pick = (div(tc, 16) == div(tr, ST)) & (rem(tc, ST) == rem(tr, ST)) & (rem(div(tc, ST), NH) == h)
        heads.append(mm(jnp.where(pick, 1.0, 0.0).astype(BF16), cd).astype(BF16))
    dctx = jnp.concatenate(heads, axis=1)
    wo_load.wait()
    for i in range(8):
        PS[i] = mm(dctx, wo[:, i * PIECE:(i + 1) * PIECE]).astype(BF16)
    rsends = []
    for i in range(1, 8):
        to = tps[i]
        c = pltpu.make_async_remote_copy(
            src_ref=PS.at[to], dst_ref=RS.at[t],
            send_sem=rs_send.at[num[i]], recv_sem=rs_recv.at[num[8 - i]],
            device_id=(g, s, to), device_id_type=MESH,
        )
        c.start()
        rsends.append(c)

    for k, p in ((5, 0), (6, 1)):
        comm(k, p)

    asends = []
    mine = tp_cols[0]

    def reduce():
        total = PS[t].astype(F32)
        for i in range(1, 8):
            frm = tps[i]
            pltpu.make_async_remote_copy(
                src_ref=PS.at[frm], dst_ref=RS.at[frm], send_sem=rs_send.at[num[0]],
                recv_sem=rs_recv.at[num[i]], device_id=(g, s, t), device_id_type=MESH,
            ).wait_recv()
            total = total + RS[frm].astype(F32)
        DO[:, :, mine] = total.reshape(DR, ST, PIECE).astype(BF16)
        for i in range(1, 8):
            c = pltpu.make_async_remote_copy(
                src_ref=DO.at[:, :, mine], dst_ref=DO.at[:, :, mine],
                send_sem=ag_send.at[num[i]], recv_sem=ag_recv.at[num[8 - i]],
                device_id=(g, s, tps[i]), device_id_type=MESH,
            )
            c.start()
            asends.append(c)

    @pl.loop(1, NS)
    def _(kk):
        j = 0
        for k in range(1, NS):
            j = j + jnp.where(kk == k, shard(*ORDER[k]), 0)

        for when, events in LATER.items():
            @pl.when(kk == when)
            def _():
                for k, p in events:
                    comm(k, p)

        @pl.when(kk == 7)
        def _():
            reduce()

        @pl.when(j < me)
        def _():
            attend(j, False)

        for when in (4, 8, 12):
            @pl.when(kk == when)
            def _():
                for k in range(when - 4, when):
                    blocks(shard(*ORDER[k]))

    for k in range(12, NS):
        blocks(shard(*ORDER[k]))
    pool_out = pltpu.make_async_copy(pool, pool_hbm, out_sem.at[0])
    pool_out.start()
    for i in range(1, 8):
        cols = tp_cols[i]
        pltpu.make_async_remote_copy(
            src_ref=DO.at[:, :, cols], dst_ref=DO.at[:, :, cols], send_sem=ag_send.at[num[0]],
            recv_sem=ag_recv.at[num[i]], device_id=(g, s, t), device_id_type=MESH,
        ).wait_recv()
    dec_out = pltpu.make_async_copy(DO, dec_hbm, out_sem.at[1])
    dec_out.start()

    for p in range(NP):
        tok = me * TOK + iota((TOK, HD), 0)
        keep = tok < len_ref[p]
        for h in range(NH):
            total = jnp.sum(L[p, h], axis=1, keepdims=True)
            out = jnp.where(keep, ACC[p, h] / total, 0.0)
            ctxs[pl.ds(p * TOK, TOK), pl.ds(h * HD, HD)] = out.astype(BF16)
    ctx_out = pltpu.make_async_copy(ctxs, ctx_hbm, out_sem.at[2])
    ctx_out.start()
    for c in sends + rsends + asends:
        c.wait_send()
    pool_out.wait()
    dec_out.wait()
    ctx_out.wait()


def deliver(ctx_in, pool_in, dec_in, ctx, pool, dec, sem):
    copies = []
    for i, (a, b) in enumerate(((ctx_in, ctx), (pool_in, pool), (dec_in, dec))):
        c = pltpu.make_async_copy(a, b, sem.at[i])
        c.start()
        copies.append(c)
    for c in copies:
        c.wait()


def tables():
    freq = THETA ** (-np.arange(HD // 2, dtype=np.float64) * 2.0 / HD)
    ang = np.arange(TOK, dtype=np.float64)[:, None] * freq[None, :]
    tab = np.zeros((2 * TOK + 8, HD), np.float32)
    tab[:TOK] = np.concatenate([np.cos(ang), np.cos(ang)], axis=1)
    tab[TOK : 2 * TOK] = np.concatenate([-np.sin(ang), np.sin(ang)], axis=1)
    tab[2 * TOK] = np.concatenate([freq, freq])
    return tab


def per_device(
    prompt_tokens, prompt_lengths, prompt_token_start, block_owner, decode_hidden,
    cache_lengths, key_cache, value_cache, w_query, w_key, w_value, w_out,
    query_gain, key_gain,
):
    sm = pl.BlockSpec(memory_space=pltpu.SMEM)
    hbm = pl.BlockSpec(memory_space=pl.ANY)
    V = pltpu.VMEM
    ctx, pool, dec = pl.pallas_call(
        kernel,
        out_shape=(
            jax.ShapeDtypeStruct((ROWS, NH * HD), BF16),
            jax.ShapeDtypeStruct((NS, HD, HD), BF16),
            jax.ShapeDtypeStruct((DR, ST, D), BF16),
        ),
        in_specs=[sm] * 4 + [hbm] * 11,
        out_specs=(hbm, hbm, hbm),
        scratch_shapes=[
            V((ROWS + DT, D), BF16),
            V((DR, ST, D), BF16),
            V((DR, CACHE, HD), BF16),
            V((DR, CACHE, HD), BF16),
            V((D, NH * HD), BF16),
            V((D, 2 * HD), BF16),
            V((NH * HD, D), BF16),
            V((ROWS + DT, 2 * HD), F32),
            V((ROWS + DT, NH * HD), F32),
            V((ROWS, HD), F32),
            V((ROWS, HD), F32),
            V((DT, HD), F32),
            V((DT, HD), F32),
            V((NS, NP, CH, HD), BF16),
            V((NP, NH, TOK, HD), BF16),
            V((NP, NH, TOK, HD), F32),
            V((NP, NH, TOK, HD), F32),
            V((NP, NH, TOK, HD), F32),
            V((DT, HD), BF16),
            V((DT, HD), BF16),
            V((DT, NH * HD), BF16),
            V((2 * TOK + 8, HD), F32),
            V((2, 1, HD), F32),
            V((HD, 4 * TOK), BF16),
            V((16, 4 * TOK), F32),
            V((NS, HD, HD), BF16),
            V((ROWS, NH * HD), BF16),
            V((8, DT, PIECE), BF16),
            V((8, DT, PIECE), BF16),
            V((DR, ST, D), BF16),
            pltpu.SemaphoreType.DMA((32,)),
            pltpu.SemaphoreType.DMA((3,)),
            pltpu.SemaphoreType.DMA((64,)),
            pltpu.SemaphoreType.DMA((64,)),
            pltpu.SemaphoreType.DMA((8,)),
            pltpu.SemaphoreType.DMA((8,)),
            pltpu.SemaphoreType.DMA((8,)),
            pltpu.SemaphoreType.DMA((8,)),
        ],
        compiler_params=pltpu.CompilerParams(
            collective_id=0, has_side_effects=True, vmem_limit_bytes=58 * 1024 * 1024
        ),
        name="split_attention",
    )(
        prompt_token_start, prompt_lengths,
        block_owner.transpose(1, 2, 0).reshape(NP, 8), cache_lengths,
        jnp.asarray(tables()),
        query_gain.reshape(1, HD), key_gain.reshape(1, HD),
        prompt_tokens.reshape(ROWS, D), decode_hidden, key_cache, value_cache,
        w_query, w_key, w_value, w_out,
    )
    ctx, pool, dec = pl.pallas_call(
        deliver,
        out_shape=(
            jax.ShapeDtypeStruct((ROWS, NH * HD), BF16),
            jax.ShapeDtypeStruct((NS, HD, HD), BF16),
            jax.ShapeDtypeStruct((DR, ST, D), BF16),
        ),
        in_specs=[pl.BlockSpec(memory_space=pltpu.VMEM)] * 3,
        out_specs=(hbm, hbm, hbm),
        scratch_shapes=[pltpu.SemaphoreType.DMA((3,))],
        name="deliver",
    )(ctx, pool, dec)
    return (
        ctx.reshape(NP, TOK, NH * HD),
        pool.reshape(1, 2 * NS, 32, 2, HD),
        dec,
    )


def solution(mesh):
    placed = (
        P(None, ("group", "seq"), None),
        P(),
        P(),
        P(("group", "seq"), None, None),
        P(("group", "seq"), None, None),
        P(("group", "seq")),
        P(("group", "seq"), None, "tp"),
        P(("group", "seq"), None, "tp"),
        P(None, "tp"),
        P(None, "tp"),
        P(None, "tp"),
        P("tp", None),
        P(),
        P(),
    )
    return jax.shard_map(
        per_device,
        mesh=mesh,
        in_specs=placed,
        out_specs=(
            P(None, ("group", "seq"), "tp"),
            P(("group", "seq"), None, None, None, "tp"),
            P(("group", "seq"), None, None),
        ),
        check_vma=False,
    )
```

time: 57.6 us -> 51.3 us (0.89)
  local copies, waits for them, and re-layouts: 5.97 us -> 0 us
    unnamed x2 -> x0, local copies, waits for them, and re-layouts: 4.14 us -> none
    pallas_call x1, Pallas kernels: 50.7 us -> 48 us  [per_device(): pl.pallas_call(kernel, out_shape=(jax.ShapeDtypeStruct((ROWS, NH * HD), B...]
    pallas_call x0 -> x1, Pallas kernels: none -> 2.38 us  [per_device(): pl.pallas_call(deliver, out_shape=(jax.ShapeDtypeStruct((ROWS, NH * HD),...]
    reshape x1 -> x0, local copies, waits for them, and re-layouts: 1.82 us -> none  [per_device(): dec.reshape(DR, ST, D)]
where the time goes in v2:
time: 51.3 us; the launch traced here: 51.2 us
  Pallas kernels  50.4 us (98%)
  between operations  0.8 us (2%)
    pallas_call x1, Pallas kernels, per_device(): pl.pallas_call(kernel, out_shape=(jax.ShapeDtypeStruct((ROWS, NH * HD), B...  48 us
    pallas_call x1, Pallas kernels, per_device(): pl.pallas_call(deliver, out_shape=(jax.ShapeDtypeStruct((ROWS, NH * HD),...  2.38 us

profile of v2, /device:TPU:30, one launch (start us, length us, event | category | flops | bytes accessed | tf_op | source)
XLA Modules:
  0.0 51.2 jit_solution(5042406911838144881)
XLA Ops:
  0.6 48.0 %split_attention.1 = (bf16[512,512]{1,0:T(8,128)(2,1)}, bf16[16,128,128]{2,1,0:T(8,128)(2,1)}, bf16[8,4,5120]{2,1,0:T(4,128)(2,1)}) custom-call(s32[2]{0:T(128)} %start_ref.1, s32[2]{0:T(128)} %len_ref.1, s32[2,8]{1,0:T(2,128)} %bitcast.9, s32[8]{0:T(128)} %clen_ref.1, f32[520,128]{1,0:T(8,128)} %constant.2.clone.tab_hbm, f32[1,128]{1,0:T(1,128)} %bitcast.10, ...), custom_call_target="tpu_custom_call" | custom-call | tf_op jit(solution)/shard_map/split_attention/pallas_call | solution.py:528
  48.6 2.4 %deliver.1 = (bf16[512,512]{1,0:T(8,128)(2,1)}, bf16[16,128,128]{2,1,0:T(8,128)(2,1)}, bf16[8,4,5120]{2,1,0:T(4,128)(2,1)}) custom-call(bf16[512,512]{1,0:T(8,128)(2,1)} %get-tuple-element.9.ctx_in, bf16[16,128,128]{2,1,0:T(8,128)(2,1)} %get-tuple-element.10.pool_in, bf16[8,4,5120]{2,1,0:T(4,128)(2,1)} %get-tuple-element.11.dec_in), custom_call_target="tpu_custom_call" | custom-call | tf_op jit(solution)/shard_map/deliver/pallas_call | solution.py:589

commit v3 on v2

--- a/solution.py
+++ b/solution.py
@@ -40,15 +40,14 @@
 ]
 STEP = {o: k for k, o in enumerate(ORDER)}
 LATER = {
-    3: ((7, 0), (8, 0), (7, 1), (8, 1)),
-    4: ((9, 0), (10, 0), (9, 1), (10, 1)),
-    5: ((5, 1),),
-    6: ((6, 0),),
-    8: ((13, 0), (14, 0), (11, 1), (12, 1)),
-    11: ((11, 0), (12, 0)),
-    13: ((13, 1), (14, 1)),
-    15: ((15, 0), (15, 1)),
+    2: ((7, 0), (8, 0), (7, 1), (8, 1)),
+    3: ((9, 0), (10, 0), (9, 1), (10, 1), (5, 1), (6, 0)),
+    4: ((13, 0), (14, 0), (11, 1), (12, 1)),
+    6: ((11, 0), (12, 0)),
+    7: ((13, 1), (14, 1)),
+    8: ((15, 0), (15, 1)),
 }
+BLOCKS = {3: range(0, 4), 5: range(4, 8), 6: range(8, 11), 8: range(11, 15)}
 
 
 def rem(a, b):
@@ -219,11 +218,6 @@
         else:
             qacc[...] += part
 
-    query_part(0)
-    query_part(1)
-    kc_load.start()
-    vc_load.start()
-
     pl.semaphore_wait(bar, 4 + 7)
 
     sends = []
@@ -293,8 +287,11 @@
     number = rem(div(col, 32), 8) * 2 + div(col, 2 * TOK)
     NUM[...] = number.astype(F32)
 
-    for i in range(2, NKC):
+    for i in range(NKC):
         query_part(i)
+        if i == 1:
+            kc_load.start()
+            vc_load.start()
         if i == 3:
             wo_load.start()
     qg = gains[0]
@@ -305,39 +302,51 @@
             Qs[p, h] = norm_rope(qacc[rows, cols], qg, cosf[rows, :], sinf[rows, :])
         dq[:, cols] = norm_rope(qacc[drows, cols], qg, dcos[...], dsin[...])
 
-    bodies = [(p, h) for p in range(NP) for h in range(NH)]
-
-    def attend(j, own):
-        def scores(p, h):
-            sc = nt(Qs[p, h], G[j, p, pl.ds(0, TOK), :])
+    def attend(shards, own, rows):
+        bodies = [(p, h, r) for p in range(NP) for h in range(NH) for r in range(0, TOK, rows)]
+
+        def scores(p, h, r):
+            at_rows = pl.ds(r, rows)
+            tiles = []
+            for j in shards:
+                sc = nt(Qs[p, h, at_rows, :], G[j, p, pl.ds(0, TOK), :])
+                if own:
+                    sc = jnp.where(iota((rows, TOK), 1) <= iota((rows, TOK), 0) + r, sc, -1e30)
+                tiles += [sc[:, :HD], sc[:, HD:]]
+            return tiles
+
+        def soft(p, h, r, tiles):
+            at_rows = pl.ds(r, rows)
+            top = tiles[0]
+            for tile in tiles[1:]:
+                top = jnp.maximum(top, tile)
+            top = jnp.max(top, axis=1, keepdims=True)
             if own:
-                sc = jnp.where(iota((TOK, TOK), 1) <= iota((TOK, TOK), 0), sc, -1e30)
-            return sc
-
-        def soft(p, h, sc):
-            s0 = sc[:, :HD]
-            s1 = sc[:, HD:]
-            top = jnp.max(jnp.maximum(s0, s1), axis=1, keepdims=True)
-            if own:
-                new = jnp.broadcast_to(top, (TOK, HD))
+                new = jnp.broadcast_to(top, (rows, HD))
             else:
-                old = M[p, h]
+                old = M[p, h, at_rows, :]
                 new = jnp.maximum(old, top)
             mb = new * SM
-            p0 = jnp.exp2(s0 * SM - mb)
-            p1 = jnp.exp2(s1 * SM - mb)
-            M[p, h] = new
+            ws = [jnp.exp2(tile * SM - mb) for tile in tiles]
+            total = ws[0]
+            for w in ws[1:]:
+                total = total + w
+            M[p, h, at_rows, :] = new
+            alpha = None
             if own:
-                L[p, h] = p0 + p1
-                alpha = None
+                L[p, h, at_rows, :] = total
             else:
                 alpha = jnp.exp2(old * SM - mb)
-                L[p, h] = L[p, h] * alpha + (p0 + p1)
-            return jnp.concatenate([p0.astype(BF16), p1.astype(BF16)], axis=1), alpha
-
-        def mix(p, h, w, alpha):
-            o = mm(w, G[j, p, pl.ds(TOK, TOK), :])
-            ACC[p, h] = o if own else ACC[p, h] * alpha + o
+                L[p, h, at_rows, :] = L[p, h, at_rows, :] * alpha + total
+            ws = [w.astype(BF16) for w in ws]
+            return [jnp.concatenate(ws[n : n + 2], axis=1) for n in range(0, len(ws), 2)], alpha
+
+        def mix(p, h, r, ws, alpha):
+            at_rows = pl.ds(r, rows)
+            o = mm(ws[0], G[shards[0], p, pl.ds(TOK, TOK), :])
+            for w, j in zip(ws[1:], shards[1:]):
+                o = o + mm(w, G[j, p, pl.ds(TOK, TOK), :])
+            ACC[p, h, at_rows, :] = o if own else ACC[p, h, at_rows, :] * alpha + o
 
         sc = scores(*bodies[0])
         waiting = None
@@ -366,7 +375,7 @@
     for k, p in ((1, 0), (2, 0), (3, 1), (4, 1)):
         comm(k, p)
 
-    attend(me, True)
+    attend((me,), True, TOK)
 
     kc_load.wait()
     vc_load.wait()
@@ -442,34 +451,42 @@
             c.start()
             asends.append(c)
 
-    @pl.loop(1, NS)
-    def _(kk):
-        j = 0
-        for k in range(1, NS):
-            j = j + jnp.where(kk == k, shard(*ORDER[k]), 0)
+    @pl.loop(1, NS // 2 + 1)
+    def _(turn):
+        ja = 0
+        jb = 0
+        for n in range(1, NS // 2 + 1):
+            ja = ja + jnp.where(turn == n, shard(*ORDER[2 * n - 1]), 0)
+            jb = jb + jnp.where(turn == n, shard(*ORDER[2 * n]) if 2 * n < NS else NS, 0)
+
+        for when, ks in BLOCKS.items():
+            @pl.when(turn == when)
+            def _():
+                for k in ks:
+                    blocks(shard(*ORDER[k]))
 
         for when, events in LATER.items():
-            @pl.when(kk == when)
+            @pl.when(turn == when)
             def _():
                 for k, p in events:
                     comm(k, p)
 
-        @pl.when(kk == 7)
+        @pl.when(turn == 4)
         def _():
             reduce()
 
-        @pl.when(j < me)
+        early = jnp.minimum(ja, jb)
+        late = jnp.maximum(ja, jb)
+
+        @pl.when(late < me)
         def _():
-            attend(j, False)
-
-        for when in (4, 8, 12):
-            @pl.when(kk == when)
-            def _():
-                for k in range(when - 4, when):
-                    blocks(shard(*ORDER[k]))
-
-    for k in range(12, NS):
-        blocks(shard(*ORDER[k]))
+            attend((early, late), False, TOK)
+
+        @pl.when((early < me) & (late >= me))
+        def _():
+            attend((early,), False, TOK)
+
+    blocks(shard(*ORDER[15]))
     pool_out = pltpu.make_async_copy(pool, pool_hbm, out_sem.at[0])
     pool_out.start()
     for i in range(1, 8):

time: 51.3 us -> 46.2 us (0.901)
  Pallas kernels: 50.4 us -> 45.2 us
    pallas_call x1, Pallas kernels: 48 us -> 42.8 us  [per_device(): pl.pallas_call(kernel, out_shape=(jax.ShapeDtypeStruct((ROWS, NH * HD), B...]
where the time goes in v3:
time: 46.2 us; the launch traced here: 46 us
  Pallas kernels  45.2 us (98%)
  between operations  0.8 us (2%)
    pallas_call x1, Pallas kernels, per_device(): pl.pallas_call(kernel, out_shape=(jax.ShapeDtypeStruct((ROWS, NH * HD), B...  42.8 us
    pallas_call x1, Pallas kernels, per_device(): pl.pallas_call(deliver, out_shape=(jax.ShapeDtypeStruct((ROWS, NH * HD),...  2.38 us

profile of v3, /device:TPU:30, one launch (start us, length us, event | category | flops | bytes accessed | tf_op | source)
XLA Modules:
  0.0 46.0 jit_solution(17259288855371895524)
XLA Ops:
  0.6 42.8 %split_attention.1 = (bf16[512,512]{1,0:T(8,128)(2,1)}, bf16[16,128,128]{2,1,0:T(8,128)(2,1)}, bf16[8,4,5120]{2,1,0:T(4,128)(2,1)}) custom-call(s32[2]{0:T(128)} %start_ref.1, s32[2]{0:T(128)} %len_ref.1, s32[2,8]{1,0:T(2,128)} %bitcast.9, s32[8]{0:T(128)} %clen_ref.1, f32[520,128]{1,0:T(8,128)} %constant.2.clone.tab_hbm, f32[1,128]{1,0:T(1,128)} %bitcast.10, ...), custom_call_target="tpu_custom_call" | custom-call | tf_op jit(solution)/shard_map/split_attention/pallas_call | solution.py:545
  43.5 2.4 %deliver.1 = (bf16[512,512]{1,0:T(8,128)(2,1)}, bf16[16,128,128]{2,1,0:T(8,128)(2,1)}, bf16[8,4,5120]{2,1,0:T(4,128)(2,1)}) custom-call(bf16[512,512]{1,0:T(8,128)(2,1)} %get-tuple-element.9.ctx_in, bf16[16,128,128]{2,1,0:T(8,128)(2,1)} %get-tuple-element.10.pool_in, bf16[8,4,5120]{2,1,0:T(4,128)(2,1)} %get-tuple-element.11.dec_in), custom_call_target="tpu_custom_call" | custom-call | tf_op jit(solution)/shard_map/deliver/pallas_call | solution.py:606

commit v4 on v3

--- a/solution.py
+++ b/solution.py
@@ -42,7 +42,7 @@
 LATER = {
     2: ((7, 0), (8, 0), (7, 1), (8, 1)),
     3: ((9, 0), (10, 0), (9, 1), (10, 1), (5, 1), (6, 0)),
-    4: ((13, 0), (14, 0), (11, 1), (12, 1)),
+    5: ((13, 0), (14, 0), (11, 1), (12, 1)),
     6: ((11, 0), (12, 0)),
     7: ((13, 1), (14, 1)),
     8: ((15, 0), (15, 1)),
@@ -320,14 +320,13 @@
             top = tiles[0]
             for tile in tiles[1:]:
                 top = jnp.maximum(top, tile)
-            top = jnp.max(top, axis=1, keepdims=True)
+            top = jnp.max(top, axis=1, keepdims=True) * SM
             if own:
                 new = jnp.broadcast_to(top, (rows, HD))
             else:
                 old = M[p, h, at_rows, :]
                 new = jnp.maximum(old, top)
-            mb = new * SM
-            ws = [jnp.exp2(tile * SM - mb) for tile in tiles]
+            ws = [jnp.exp2(tile * SM - new) for tile in tiles]
             total = ws[0]
             for w in ws[1:]:
                 total = total + w
@@ -336,7 +335,7 @@
             if own:
                 L[p, h, at_rows, :] = total
             else:
-                alpha = jnp.exp2(old * SM - mb)
+                alpha = jnp.exp2(old - new)
                 L[p, h, at_rows, :] = L[p, h, at_rows, :] * alpha + total
             ws = [w.astype(BF16) for w in ws]
             return [jnp.concatenate(ws[n : n + 2], axis=1) for n in range(0, len(ws), 2)], alpha
@@ -390,9 +389,12 @@
     sn = nt(qd, dk[...])
     sn = jnp.where(same & (rem(ec, ST) <= rem(er, ST)), sn, -1e30)
     outs = []
+    ahead = [nt(qd[:16], kc[0]), nt(qd[16:32], kc[1])]
     for r in range(DR):
         span = slice(r * 16, r * 16 + 16)
-        sr = nt(qd[span], kc[r])
+        if r + 2 < DR:
+            ahead.append(nt(qd[r * 16 + 32 : r * 16 + 48], kc[r + 2]))
+        sr = ahead[r]
         sr = jnp.where(iota((16, CACHE), 1) < clen_ref[r], sr, -1e30)
         top = jnp.maximum(
             jnp.max(sr, axis=1, keepdims=True), jnp.max(sn[span], axis=1, keepdims=True)
@@ -471,7 +473,7 @@
                 for k, p in events:
                     comm(k, p)
 
-        @pl.when(turn == 4)
+        @pl.when(turn == 5)
         def _():
             reduce()
 
@@ -498,6 +500,7 @@
     dec_out = pltpu.make_async_copy(DO, dec_hbm, out_sem.at[1])
     dec_out.start()
 
+    ctx_outs = []
     for p in range(NP):
         tok = me * TOK + iota((TOK, HD), 0)
         keep = tok < len_ref[p]
@@ -505,23 +508,33 @@
             total = jnp.sum(L[p, h], axis=1, keepdims=True)
             out = jnp.where(keep, ACC[p, h] / total, 0.0)
             ctxs[pl.ds(p * TOK, TOK), pl.ds(h * HD, HD)] = out.astype(BF16)
-    ctx_out = pltpu.make_async_copy(ctxs, ctx_hbm, out_sem.at[2])
-    ctx_out.start()
+        rows = pl.ds(p * TOK, TOK)
+        ctx_outs.append(pltpu.make_async_copy(ctxs.at[rows], ctx_hbm.at[rows], out_sem.at[2 + p]))
+        ctx_outs[p].start()
     for c in sends + rsends + asends:
         c.wait_send()
     pool_out.wait()
     dec_out.wait()
-    ctx_out.wait()
-
-
-def deliver(ctx_in, pool_in, dec_in, ctx, pool, dec, sem):
-    copies = []
-    for i, (a, b) in enumerate(((ctx_in, ctx), (pool_in, pool), (dec_in, dec))):
-        c = pltpu.make_async_copy(a, b, sem.at[i])
+    for c in ctx_outs:
+        c.wait()
+
+
+def deliver(ctx_in, pool_in, dec_in, ctx, pool, dec, ctx_v, pool_v, dec_v, rsem, wsem):
+    reads = []
+    writes = []
+    for i, (a, v, b) in enumerate(((ctx_in, ctx_v, ctx), (pool_in, pool_v, pool), (dec_in, dec_v, dec))):
+        half = a.shape[0] // 2
+        for n in range(2):
+            part = pl.ds(n * half, half)
+            reads.append(pltpu.make_async_copy(a.at[part], v.at[part], rsem.at[2 * i + n]))
+            writes.append(pltpu.make_async_copy(v.at[part], b.at[part], wsem.at[2 * i + n]))
+    for c in reads:
         c.start()
-        copies.append(c)
-    for c in copies:
+    for c, w in zip(reads, writes):
         c.wait()
+        w.start()
+    for w in writes:
+        w.wait()
 
 
 def tables():
@@ -583,7 +596,7 @@
             V((8, DT, PIECE), BF16),
             V((DR, ST, D), BF16),
             pltpu.SemaphoreType.DMA((32,)),
-            pltpu.SemaphoreType.DMA((3,)),
+            pltpu.SemaphoreType.DMA((4,)),
             pltpu.SemaphoreType.DMA((64,)),
             pltpu.SemaphoreType.DMA((64,)),
             pltpu.SemaphoreType.DMA((8,)),
@@ -610,9 +623,16 @@
             jax.ShapeDtypeStruct((NS, HD, HD), BF16),
             jax.ShapeDtypeStruct((DR, ST, D), BF16),
         ),
-        in_specs=[pl.BlockSpec(memory_space=pltpu.VMEM)] * 3,
+        in_specs=[hbm] * 3,
         out_specs=(hbm, hbm, hbm),
-        scratch_shapes=[pltpu.SemaphoreType.DMA((3,))],
+        scratch_shapes=[
+            V((ROWS, NH * HD), BF16),
+            V((NS, HD, HD), BF16),
+            V((DR, ST, D), BF16),
+            pltpu.SemaphoreType.DMA((6,)),
+            pltpu.SemaphoreType.DMA((6,)),
+        ],
+        compiler_params=pltpu.CompilerParams(vmem_limit_bytes=58 * 1024 * 1024),
         name="deliver",
     )(ctx, pool, dec)
     return (

time: 46.2 us -> 45.3 us (0.981); the launches traced: 46 us -> 44.5 us
  Pallas kernels: 45.2 us -> 43.7 us
    pallas_call x1, Pallas kernels: 42.8 us -> 41.6 us  [per_device(): pl.pallas_call(kernel, out_shape=(jax.ShapeDtypeStruct((ROWS, NH * HD), B...]
where the time goes in v4:
time: 45.3 us; the launch traced here: 44.5 us
  Pallas kernels  43.7 us (96%)
  between operations  0.8 us (2%)
    pallas_call x1, Pallas kernels, per_device(): pl.pallas_call(kernel, out_shape=(jax.ShapeDtypeStruct((ROWS, NH * HD), B...  41.6 us
    pallas_call x1, Pallas kernels, per_device(): pl.pallas_call(deliver, out_shape=(jax.ShapeDtypeStruct((ROWS, NH * HD),...  2.12 us

profile of v4, /device:TPU:30, one launch (start us, length us, event | category | flops | bytes accessed | tf_op | source)
XLA Modules:
  0.0 44.5 jit_solution(557927942858685386)
XLA Ops:
  0.6 41.6 %split_attention.1 = (bf16[512,512]{1,0:T(8,128)(2,1)}, bf16[16,128,128]{2,1,0:T(8,128)(2,1)}, bf16[8,4,5120]{2,1,0:T(4,128)(2,1)}) custom-call(s32[2]{0:T(128)} %start_ref.1, s32[2]{0:T(128)} %len_ref.1, s32[2,8]{1,0:T(2,128)} %bitcast.9, s32[8]{0:T(128)} %clen_ref.1, f32[520,128]{1,0:T(8,128)} %constant.2.clone.tab_hbm, f32[1,128]{1,0:T(1,128)} %bitcast.10, ...), custom_call_target="tpu_custom_call" | custom-call | tf_op jit(solution)/shard_map/split_attention/pallas_call | solution.py:558
  42.3 2.1 %deliver.1 = (bf16[512,512]{1,0:T(8,128)(2,1)}, bf16[16,128,128]{2,1,0:T(8,128)(2,1)}, bf16[8,4,5120]{2,1,0:T(4,128)(2,1)}) custom-call(bf16[512,512]{1,0:T(8,128)(2,1)} %get-tuple-element.9.ctx_in, bf16[16,128,128]{2,1,0:T(8,128)(2,1)} %get-tuple-element.10.pool_in, bf16[8,4,5120]{2,1,0:T(4,128)(2,1)} %get-tuple-element.11.dec_in), custom_call_target="tpu_custom_call" | custom-call | tf_op jit(solution)/shard_map/deliver/pallas_call | solution.py:619
